TPU v7x, 32 devices: a whole 2x2x4 slice. The times are simulated.
32 devices in a mesh: blocks: 2 (over x), pencil: 4 (over y, core), tile: 4 (over z).
Axes of the slice: x: 2, y: 2, z: 4, core: 2. Of those that a mesh axis runs over, the one named last changes fastest.
Arguments:
- right_face: bfloat16 [8, 2, 2048, 2048], P(('blocks', 'tile'), None, 'pencil'), parts along dimension 0, may hold values from -6 to 6
- left_face: bfloat16 [8, 2, 2048, 2048], P(('blocks', 'tile'), None, 'pencil'), parts along dimension 0, may hold values from -6 to 6
- intersection_list: int32 [8, 3], P(('blocks', 'tile')), parts along dimension 0, may hold values from -64 to 64, as said below
- slice_ranges: int32 [8, 2], P(('blocks', 'tile')), parts along dimension 0, may hold values from 0 to 1, as said below
Outputs:
- maps: float32 [8, 2, 2048, 2048], P(('blocks', 'tile'), None, 'pencil'), parts along dimension 0
There are 2 independent parts, one for each index of `blocks`. A program takes and returns all parts, laid end to end along the dimension named above; each array names one. Nothing has to cross between parts.
Inputs may be any that keep to these rules, and one draw needn't show every extreme that they name: `intersection_list`: column 0 is the intersection's width in slices, 1 to 2; it is 2 for some intersection and 1 for another. Columns 1 and 2 are coarse row and column offsets in pixels. `slice_ranges`: each first slice plus the intersection's width is at most 2.
All inputs are finite; a program needn't handle non-finite values.
Results may differ from a plain program's by a relative error of at most 0.0003.
Values may be sent and summed in bfloat16 or wider, within the bound.
A program may use at most 192 MiB of HBM per device.

v0:
```python
import math

import jax
import jax.numpy as jnp
from jax import lax
from jax.sharding import PartitionSpec as P

REG = 0.25
precision_mode = lax.Precision.HIGHEST


def from_behind(value, axis, steps):
    count = lax.axis_size(axis)
    pairs = [(source, (source + steps) % count) for source in range(count)]
    return lax.ppermute(value, axis, pairs)


def split_len(length):
    factor = 128
    while length % factor != 0 or factor >= length:
        factor = factor // 2
    return (length // factor, factor)


def make_table(modulus, first, second, sign):
    rows_index = jnp.arange(first, dtype=jnp.int32)[:, None]
    cols_index = jnp.arange(second, dtype=jnp.int32)[None, :]
    angle = (rows_index * cols_index % modulus).astype(jnp.float32) * (2.0 * math.pi / modulus)
    return (jnp.cos(angle), sign * jnp.sin(angle))


def block_table(modulus, sign):
    cos_part, sin_part = make_table(modulus, modulus, modulus, sign)
    return jnp.stack([jnp.stack([cos_part, sin_part]), jnp.stack([0.0 - sin_part, cos_part])])


def factor_shape(initial, along_last):
    length = initial[-1] if along_last else initial[-2]
    p, q = split_len(length)
    if along_last:
        return (length, p, q, initial[:-1] + (p, q), "")
    return (length, p, q, initial[:-2] + (p, q, initial[-1]), "c")


def apply_twist(values, length, p, q, along_last, sign):
    twist_real, twist_imag = make_table(length, p, q, sign)
    if not along_last:
        twist_real = twist_real[:, :, None]
        twist_imag = twist_imag[:, :, None]
    return jnp.stack(
        [
            values[0] * twist_real - values[1] * twist_imag,
            values[0] * twist_imag + values[1] * twist_real,
        ]
    )


def forward_dft(values, along_last, real_input):
    tail = values.shape if real_input else values.shape[1:]
    length, p, q, new_tail, suffix = factor_shape(tail, along_last)
    first = block_table(p, -1.0)
    if real_input:
        values = values.reshape(new_tail)
        values = jnp.einsum(
            "...pq" + suffix + ",tpk->t...kq" + suffix, values, first[0], precision=precision_mode
        )
    else:
        values = values.reshape((2,) + new_tail)
        values = jnp.einsum(
            "s...pq" + suffix + ",stpk->t...kq" + suffix, values, first, precision=precision_mode
        )
    values = apply_twist(values, length, p, q, along_last, -1.0)
    second = block_table(q, -1.0)
    values = jnp.einsum(
        "s...kq" + suffix + ",stql->t...kl" + suffix, values, second, precision=precision_mode
    )
    return values.reshape((2,) + tail)


def inverse_dft(values, along_last, real_only):
    tail = values.shape[1:]
    length, p, q, new_tail, suffix = factor_shape(tail, along_last)
    values = values.reshape((2,) + new_tail)
    first = block_table(q, 1.0)
    values = jnp.einsum(
        "s...pq" + suffix + ",stqm->t...pm" + suffix, values, first, precision=precision_mode
    )
    values = apply_twist(values, length, p, q, along_last, 1.0)
    last = block_table(p, 1.0)
    if real_only:
        result = jnp.einsum(
            "s...pm" + suffix + ",spr->...rm" + suffix, values, last[:, 0], precision=precision_mode
        )
        return result.reshape(tail)
    values = jnp.einsum(
        "s...pm" + suffix + ",stpr->t...rm" + suffix, values, last, precision=precision_mode
    )
    return values.reshape((2,) + tail)


def column_pass(parts):
    return forward_dft(parts, False, False)


def spectrum(pixels):
    row_spec = forward_dft(pixels.astype(jnp.float32), True, True)
    return column_pass(lax.all_to_all(row_spec, "pencil", split_axis=3, concat_axis=2, tiled=True))


def cross_power(near, far, scale):
    prod_real = near[0] * far[0] + near[1] * far[1]
    prod_imag = near[1] * far[0] - near[0] * far[1]
    weight = 1.0 / (jnp.sqrt(prod_real * prod_real + prod_imag * prod_imag) + scale)
    return jnp.stack([prod_real * weight, prod_imag * weight])


def frequencies(positions, length):
    p, q = split_len(length)
    return positions // q + p * (positions % q)


def shards(right_face, left_face, intersection_list, slice_ranges):
    right_slices = right_face[0]
    left_slices = left_face[0]
    depth = right_slices.shape[0]
    width = right_slices.shape[-1]
    height = right_slices.shape[1] * lax.axis_size("pencil")
    columns = width // lax.axis_size("pencil")
    scale = REG * height * width
    live_count = intersection_list[0, 0]
    shift_rows = intersection_list[0, 1]
    shift_cols = intersection_list[0, 2]
    start_near = slice_ranges[0, 0]
    start_far = slice_ranges[0, 1]
    moved_spectra = from_behind(spectrum(left_slices), "tile", -1)
    slice_steps = jnp.arange(depth, dtype=jnp.int32)
    near_spec = spectrum(
        jnp.take(right_slices, jnp.minimum(start_near + slice_steps, depth - 1), axis=0)
    )
    far_spec = jnp.take(moved_spectra, jnp.minimum(start_far + slice_steps, depth - 1), axis=1)
    power = cross_power(near_spec, far_spec, scale)
    live = (slice_steps < live_count).astype(jnp.float32)[None, :, None, None]
    total = jnp.sum(power * live, axis=1)
    inverse_count = 1.0 / live_count.astype(jnp.float32)
    mean_real = total[0] * inverse_count
    mean_imag = total[1] * inverse_count
    row_freq = frequencies(jnp.arange(height, dtype=jnp.int32), height)[:, None]
    col_freq = frequencies(
        lax.axis_index("pencil") * columns + jnp.arange(columns, dtype=jnp.int32), width
    )[None, :]
    angle = (row_freq * shift_rows % height).astype(jnp.float32) * (2.0 * math.pi / height) + (
        col_freq * shift_cols % width
    ).astype(jnp.float32) * (2.0 * math.pi / width)
    rotated = jnp.stack(
        [
            mean_real * jnp.cos(angle) - mean_imag * jnp.sin(angle),
            mean_real * jnp.sin(angle) + mean_imag * jnp.cos(angle),
        ]
    )
    col_spec = inverse_dft(rotated, False, False)
    back_spec = lax.all_to_all(col_spec, "pencil", split_axis=1, concat_axis=2, tiled=True)
    own_map = inverse_dft(back_spec, True, True) * (1.0 / math.sqrt(height * width))
    other_map = from_behind(own_map, "tile", 1)
    return jnp.stack([own_map, other_map])[None]


def solution(mesh):
    placed = (
        P(("blocks", "tile"), None, "pencil", None),
        P(("blocks", "tile"), None, "pencil", None),
        P(("blocks", "tile"), None),
        P(("blocks", "tile"), None),
    )
    return jax.shard_map(
        shards,
        mesh=mesh,
        in_specs=placed,
        out_specs=P(("blocks", "tile"), None, "pencil", None),
        check_vma=False,
    )
```

profile of v0, /device:TPU:0, one launch (start us, length us, event | category | flops | bytes accessed | tf_op | source)
XLA Modules:
  0.0 1409.6 jit_solution(15904922097916823752)
XLA Ops:
  0.1 1.3 fusion.134
  3.6 4.7 fusion.132
  8.3 2.3 gather_fusion
  10.6 3.6 gather_fusion.1
  14.2 2.2 pad_maximum_fusion.6
  16.4 1.4 copy.157
  17.8 1.4 copy.158
  19.2 9.5 convolution_bitcast_fusion
  28.7 9.5 convolution_bitcast_fusion.1
  38.2 21.3 %multiply_subtract_fusion.2 = (f32[1,2,512,16,128]{4,3,2,1,0:T(8,128)}, f32[1,2,512,16,128]{4,3,2,1,0:T(8,128)}, f32[1,2,512,16,128]{4,3,2,1,0:T(8,128)S(1)}, f32[1,2,512,16,128]{4,3,2,1,0:T(8,128)}) fusion(f32[2,2,512,16,128]{4,3,2,1,0:T(8,128)} %convolution_bitcast_fusion, f32[16,128]{1,0:T(8,128)S(1)} %get-tuple-element.47, ...), kind=kLoop, calls=%fused_computation.50 | loop fusion | flops 25165824 | bytes 67125248 | tf_op jit(solution)/shard_map/sub | solution.py:52
  59.5 9.5 pad_maximum_fusion
  69.0 0.7 fusion.59
  69.7 28.0 %fusion.11 = f32[2,128,2,512,16,1]{3,1,5,4,2,0:T(8,128)} fusion(f32[2,2,512,16,128]{4,3,2,1,0:T(8,128)} %pad_maximum_fusion, f32[1,2,128,128]{2,3,0,1:T(8,128)S(1)} %get-tuple-element.31, f32[1,2,128,128]{2,3,0,1:T(8,128)S(1)} %get-tuple-element.32), kind=kOutput, calls=%fused_computation.22 | convolution fusion | flops 12884967424 | bytes 33816576 | tf_op jit(solution)/shard_map/s...kq,stql->t...kl/dot_general | solution.py:74
  97.8 28.6 %copy.98 = f32[2,2,512,2048]{2,1,0,3:T(2,128)} copy(f32[2,2,512,2048]{2,3,1,0:T(8,128)} %bitcast.212) | data formatting | bytes 33554432 | tf_op jit(solution)/shard_map/reshape | solution.py:77
  126.4 7.4 all-to-all-start
  133.8 11.3 pad_maximum_fusion.2
  145.1 27.8 %fusion.5 = f32[2,128,2,512,16,1]{3,1,5,4,2,0:T(8,128)} fusion(f32[2,2,512,16,128]{4,3,2,1,0:T(8,128)} %pad_maximum_fusion.2, f32[1,2,128,128]{2,3,0,1:T(8,128)S(1)} %get-tuple-element.31, f32[1,2,128,128]{2,3,0,1:T(8,128)S(1)} %get-tuple-element.32), kind=kOutput, calls=%fused_computation.16 | convolution fusion | flops 12884967424 | bytes 33816576 | tf_op jit(solution)/shard_map/s...kq,stql->t...kl/dot_general | solution.py:74
  172.9 28.8 %copy.107 = f32[2,2,512,2048]{2,1,0,3:T(2,128)} copy(f32[2,2,512,2048]{2,3,1,0:T(8,128)} %bitcast.213) | data formatting | bytes 33554432 | tf_op jit(solution)/shard_map/reshape | solution.py:77
  201.7 115.8 %all-to-all-done = f32[2,2,512,2048]{2,1,0,3:T(2,128)} async-done(((f32[2,2,512,2048]{2,1,0,3:T(2,128)}), f32[2,2,512,2048]{2,1,0,3:T(2,128)}, u32[]{:S(2)}, u32[]{:S(2)}) %all-to-all-start) | async-done | bytes 16777248 | tf_op jit(solution)/shard_map/all_to_all | solution.py:107
  317.4 7.1 all-to-all-start.1
  325.5 14.1 %copy.99 = f32[2,2,512,2048]{2,3,1,0:T(8,128)} copy(f32[2,2,512,2048]{2,1,0,3:T(2,128)} %all-to-all-done) | data formatting | bytes 33554432 | tf_op jit(solution)/shard_map/all_to_all | solution.py:107
  339.6 19.2 %copy.100 = f32[2,2,4,512,512]{4,3,2,1,0:T(8,128)} copy(f32[2,2,4,512,512]{3,4,2,1,0:T(8,128)} %bitcast.214) | data formatting | bytes 33554432 | tf_op jit(solution)/shard_map/all_to_all | solution.py:107
  358.9 148.8 %all-to-all-done.1 = f32[2,2,512,2048]{2,1,0,3:T(2,128)} async-done(((f32[2,2,512,2048]{2,1,0,3:T(2,128)}), f32[2,2,512,2048]{2,1,0,3:T(2,128)}, u32[]{:S(2)}, u32[]{:S(2)}) %all-to-all-start.1) | async-done | bytes 16777248 | tf_op jit(solution)/shard_map/all_to_all | solution.py:107
  507.6 14.1 %copy.108 = f32[2,2,512,2048]{2,3,1,0:T(8,128)} copy(f32[2,2,512,2048]{2,1,0,3:T(2,128)} %all-to-all-done.1) | data formatting | bytes 33554432 | tf_op jit(solution)/shard_map/all_to_all | solution.py:107
  521.7 19.2 %copy.109 = f32[2,2,4,512,512]{4,3,2,1,0:T(8,128)} copy(f32[2,2,4,512,512]{3,4,2,1,0:T(8,128)} %bitcast.215) | data formatting | bytes 33554432 | tf_op jit(solution)/shard_map/all_to_all | solution.py:107
  540.9 32.6 %fusion.29 = f32[2,2,16,128,512]{4,2,3,1,0:T(8,128)} fusion(f32[2,2,16,128,512]{4,3,2,1,0:T(8,128)} %bitcast.210, f32[1,2,16,16]{2,3,1,0:T(8,128)S(1)} %get-tuple-element.37, f32[1,2,16,16]{2,3,1,0:T(8,128)S(1)} %get-tuple-element.38), kind=kOutput, calls=%fused_computation.55 | convolution fusion | flops 1610613760 | bytes 33558528 | tf_op jit(solution)/shard_map/s...pqc,stpk->t...kqc/dot_general | solution.py:69
  573.6 33.1 %fusion.35 = f32[2,2,16,128,512]{4,2,3,1,0:T(8,128)} fusion(f32[2,2,16,128,512]{4,3,2,1,0:T(8,128)} %bitcast.211, f32[1,2,16,16]{2,3,1,0:T(8,128)S(1)} %get-tuple-element.37, f32[1,2,16,16]{2,3,1,0:T(8,128)S(1)} %get-tuple-element.38), kind=kOutput, calls=%fused_computation.57 | convolution fusion | flops 1610613760 | bytes 33558528 | tf_op jit(solution)/shard_map/s...pqc,stpk->t...kqc/dot_general | solution.py:69
  606.7 23.0 %multiply_subtract_fusion.1 = (f32[1,2,16,128,512]{4,2,3,1,0:T(8,128)S(1)}, f32[1,2,16,128,512]{4,2,3,1,0:T(8,128)}, f32[1,2,16,128,512]{4,2,3,1,0:T(8,128)}, f32[1,2,16,128,512]{4,2,3,1,0:T(8,128)}) fusion(f32[2,2,16,128,512]{4,2,3,1,0:T(8,128)} %fusion.35, f32[16,128]{0,1:T(8,128)S(1)} %copy.104, f32[16,128]{0,1:T(8,128)S(1)} %copy.103, ...), kind=kLoop, calls=%fused_computation.48 | loop fusion | flops 25165824 | bytes 67125248 | tf_op jit(solution)/shard_map/sub | solution.py:52
  629.7 5.0 pad_maximum_fusion.3
  634.7 23.9 %fusion.1 = f32[2,128,2,16,512,1]{4,1,5,3,2,0:T(8,128)} fusion(f32[2,2,16,128,512]{4,2,3,1,0:T(8,128)S(1)} %pad_maximum_fusion.3, f32[1,2,128,128]{2,3,0,1:T(8,128)S(1)} %get-tuple-element.31, f32[1,2,128,128]{2,3,0,1:T(8,128)S(1)} %get-tuple-element.32), kind=kOutput, calls=%fused_computation.12 | convolution fusion | flops 12884967424 | bytes 33816576 | tf_op jit(solution)/shard_map/s...kqc,stql->t...klc/dot_general | solution.py:74
  658.6 4.4 collective-permute-start
  667.7 6.9 pad_maximum_fusion.1
  674.6 29.0 %fusion.32 = f32[2,2,16,128,512]{4,3,2,1,0:T(8,128)S(1)} fusion(f32[2,2,16,128,512]{4,2,3,1,0:T(8,128)S(1)} %pad_maximum_fusion.1, f32[1,2,128,128]{2,3,0,1:T(8,128)S(1)} %get-tuple-element.31, f32[1,2,128,128]{2,3,0,1:T(8,128)S(1)} %get-tuple-element.32), kind=kOutput, calls=%fused_computation.56 | convolution fusion | flops 12884967424 | bytes 33816576 | tf_op jit(solution)/shard_map/s...kqc,stql->t...klc/dot_general | solution.py:74
  703.6 7.0 fusion.130
  710.6 312.1 %collective-permute-done = f32[2,2,2048,512]{3,2,1,0:T(8,128)} collective-permute-done((f32[2,2,2048,512]{3,2,1,0:T(8,128)}, f32[2,2,2048,512]{3,2,1,0:T(8,128)}, u32[]{:S(2)}, u32[]{:S(2)}) %collective-permute-start) | collective-permute-done | bytes 16777248 | tf_op jit(solution)/shard_map/ppermute | solution.py:15
  1022.6 10.7 fusion.131
  1033.3 6.4 gather_fusion.2
  1039.7 6.4 gather_fusion.3
  1046.0 4.6 mini-gather-slice.9
  1050.6 5.0 gather_fusion.4
  1055.6 11.9 maximum_select_fusion
  1067.5 21.5 %fusion.28 = (f32[1,2,2048,512]{3,2,0,1:T(8,128)}, f32[1,2,2048,512]{3,2,0,1:T(8,128)}, f32[1,2,2048,512]{3,2,0,1:T(8,128)}) fusion(f32[1,2,2048,512]{3,2,0,1:T(8,128)} %bitcast.219, f32[2,2,2048,512]{3,2,0,1:T(8,128)} %maximum_select_fusion, f32[1,2,2048,512]{3,2,0,1:T(8,128)} %bitcast.218), kind=kLoop, calls=%fused_computation.44 | loop fusion | flops 25165824 | bytes 58720256 | tf_op jit(solution)/shard_map/mul | solution.py:114
  1089.0 8.0 fusion.27
  1097.2 4.0 fusion
  1101.2 16.3 %fusion.42 = (f32[1,2048,512]{2,1,0:T(8,128)S(1)}, f32[1,2048,512]{2,1,0:T(8,128)S(1)}) fusion(f32[2,2048,512]{2,1,0:T(8,128)S(1)} %fusion, f32[512]{0:T(512)S(1)} %fusion.116, f32[2048]{0:T(1024)S(1)} %fusion.98, f32[]{:T(128)S(6)} %div.33), kind=kLoop, calls=%fused_computation.66 | loop fusion | flops 9437184 | bytes 16787460 | tf_op jit(solution)/shard_map/sub | solution.py:156
  1117.6 7.7 fusion.53
  1125.3 1.5 multiply_subtract_fusion.6
  1126.8 1.6 pad_maximum_fusion.4
  1128.4 12.7 fusion.50
  1141.1 4.9 copy.120
  1146.0 11.9 copy.121
  1157.9 95.9 %all_to_all.45 = f32[2,2048,512]{2,0,1:T(2,128)S(1)} all-to-all(f32[2,2048,512]{2,0,1:T(2,128)S(1)} %copy.121), channel_id=1, replica_groups=mesh['blocks'=2,'pencil'=4,'tile'=4] {'pencil'}, dimensions={1} | all-to-all | bytes 16777216 | tf_op jit(solution)/shard_map/all_to_all | solution.py:161
  1253.7 4.9 copy.122
  1258.7 10.0 copy.123
  1268.6 9.7 fusion.47
  1278.3 1.1 multiply_subtract_fusion.5
  1279.5 4.4 pad_maximum_fusion.5
  1283.9 10.4 copy.126
  1294.2 6.4 bitcast_multiply_fusion
  1300.7 2.0 copy-done
  1302.7 4.0 copy.211
  1307.1 4.9 mul.1140
  1312.0 89.4 %collective-permute-done.1 = f32[512,2048]{1,0:T(8,128)} collective-permute-done((f32[512,2048]{1,0:T(8,128)}, f32[512,2048]{1,0:T(8,128)}, u32[]{:S(2)}, u32[]{:S(2)}) %collective-permute-start.1) | collective-permute-done | bytes 4194336 | tf_op jit(solution)/shard_map/ppermute | solution.py:15
  1401.5 8.0 maximum_bitcast_fusion.2
  (41 shorter events, 7.9 us)
Async XLA Ops:
  2.8 321.8 %copy-start.5 = (f32[16,128]{1,0:T(8,128)}, f32[16,128]{1,0:T(8,128)S(1)}, u32[]{:S(2)}) copy-start(f32[16,128]{1,0:T(8,128)S(1)} %get-tuple-element.48) | copy-start | bytes 24580
  14.2 3.7 copy-start.2
  126.4 191.1 %all-to-all-start = ((f32[2,2,512,2048]{2,1,0,3:T(2,128)}), f32[2,2,512,2048]{2,1,0,3:T(2,128)}, u32[]{:S(2)}, u32[]{:S(2)}) async-start(f32[2,2,512,2048]{2,1,0,3:T(2,128)} %copy.98), calls=%async_computation | async-start | bytes 33554432 | tf_op jit(solution)/shard_map/all_to_all | solution.py:107
  317.4 190.2 %all-to-all-start.1 = ((f32[2,2,512,2048]{2,1,0,3:T(2,128)}), f32[2,2,512,2048]{2,1,0,3:T(2,128)}, u32[]{:S(2)}, u32[]{:S(2)}) async-start(f32[2,2,512,2048]{2,1,0,3:T(2,128)} %copy.107), calls=%async_computation.1 | async-start | bytes 33554432 | tf_op jit(solution)/shard_map/all_to_all | solution.py:107
  634.7 28.3 %copy-start.9 = (s32[1,3]{1,0:T(1,128)S(1)}, s32[1,3]{1,0:T(1,128)}, u32[]{:S(2)}) copy-start(s32[1,3]{1,0:T(1,128)} %param.6) | copy-start | bytes 40
  658.6 364.0 %collective-permute-start = (f32[2,2,2048,512]{3,2,1,0:T(8,128)}, f32[2,2,2048,512]{3,2,1,0:T(8,128)}, u32[]{:S(2)}, u32[]{:S(2)}) collective-permute-start(f32[2,2,2048,512]{3,2,1,0:T(8,128)} %bitcast.65), channel_id=1, source_target_pairs={{0,3},{1,0},{2,1},{3,2},{4,7},{5,4},{6,5},{7,6},{8,11},{9,8},{10,9... | collective-permute-start | bytes 50331656 | tf_op jit(solution)/shard_map/ppermute | solution.py:15
  1089.0 8.2 copy-start.1
  1101.2 16.4 %copy-start.3 = (f32[1,2,128,128]{2,3,1,0:T(8,128)S(1)}, f32[1,2,128,128]{2,3,1,0:T(8,128)}, u32[]{:S(2)}) copy-start(f32[1,2,128,128]{2,3,1,0:T(8,128)} %get-tuple-element.30) | copy-start | bytes 393220
  1101.2 16.4 %copy-start.4 = (f32[1,2,128,128]{2,3,1,0:T(8,128)S(1)}, f32[1,2,128,128]{2,3,1,0:T(8,128)}, u32[]{:S(2)}) copy-start(f32[1,2,128,128]{2,3,1,0:T(8,128)} %get-tuple-element.33) | copy-start | bytes 393220
  1117.6 7.7 copy-start.6
  1126.8 1.6 copy-start.7
  1126.8 1.6 copy-start.8
  1300.7 2.0 copy-start
  1306.7 94.8 %collective-permute-start.1 = (f32[512,2048]{1,0:T(8,128)}, f32[512,2048]{1,0:T(8,128)}, u32[]{:S(2)}, u32[]{:S(2)}) collective-permute-start(f32[512,2048]{1,0:T(8,128)} %bitcast.206), channel_id=1, source_target_pairs={{0,1},{1,2},{2,3},{3,0},{4,5},{5,6},{6,7},{7,4},{8,9},{9,10},{10,1... | collective-permute-start | bytes 12582920 | tf_op jit(solution)/shard_map/ppermute | solution.py:15
where the time goes:
time: 1420 us; the launch traced here: 1410 us
  waiting for transfers between devices  666 us (47%)
  local copies, waits for them, and re-layouts  233 us (16%)
  matrix products  230 us (16%)
  other arithmetic  164 us (12%)
  blocking collectives  95.9 us (7%)
  starting transfers between devices  19.4 us (1%)
    ppermute x2, waiting for transfers between devices, from_behind(): return lax.ppermute(value, axis, pairs)  402 us
    all_to_all x2, waiting for transfers between devices, spectrum(): lax.all_to_all(row_spec, 'pencil', split_axis=3, concat_axis=2, tiled=True)  265 us
    dot_general x4, matrix products, forward_dft(): jnp.einsum('s...kq' + suffix + ',stql->t...kl' + suffix, values, second,...  109 us
    all_to_all x1, blocking collectives, shards(): lax.all_to_all(col_spec, 'pencil', split_axis=1, concat_axis=2, tiled=True)  95.9 us
    all_to_all x4, local copies, waits for them, and re-layouts, spectrum(): lax.all_to_all(row_spec, 'pencil', split_axis=3, concat_axis=2, tiled=True)  66.7 us
    dot_general x2, matrix products, forward_dft(): jnp.einsum('s...pq' + suffix + ',stpk->t...kq' + suffix, values, first, p...  65.8 us
    reshape x2, local copies, waits for them, and re-layouts, forward_dft(): return values.reshape((2,) + tail)  57.4 us
    sub x4, other arithmetic, apply_twist(): values[0] * twist_real - values[1] * twist_imag  47 us
  transfers between devices with their start and end apart: 4, of which 4 were waited for; matrix products, arithmetic and copies ran while one was open for 11% of the time, Pallas kernels for 0%

commit v1 on v0

v1 whole, which is shorter than its diff:
```python
import math

import jax
import jax.numpy as jnp
import ml_dtypes
import numpy as np
from jax import lax
from jax.sharding import PartitionSpec as P

REG = 0.25
CHUNKS = 2
HIGH = lax.Precision.HIGH


def shift_tile(value, steps):
    count = lax.axis_size("tile")
    return lax.ppermute(value, "tile", [(s, (s + steps) % count) for s in range(count)])


def swap_groups(value, members):
    count = 2 * members
    return lax.ppermute(value, "pencil", [(s, (s + members) % count) for s in range(count)])


def shift_members(value, members, steps):
    pairs = [
        (g * members + s, g * members + (s + steps) % members)
        for g in range(2)
        for s in range(members)
    ]
    return lax.ppermute(value, "pencil", pairs)


def hi_lo(table):
    high = table.astype(ml_dtypes.bfloat16)
    low = (table - high.astype(np.float64)).astype(ml_dtypes.bfloat16)
    return jnp.asarray(high), jnp.asarray(low)


def row_tables(width, members):
    half = width // 2
    columns = half // members
    x = np.arange(width)[:, None]
    l = np.arange(half)[None, :]
    angle = (x * l % width) * (2.0 * math.pi / width)
    cos_part, sin_part = np.cos(angle), -np.sin(angle)
    sin_part[:, 0] = 1.0 - 2.0 * (np.arange(width) % 2)
    forward = np.stack([cos_part, sin_part], axis=1)
    forward = forward.reshape(width, 2, members, columns).transpose(2, 0, 1, 3)
    forward = forward.reshape(members, width, 2 * columns)
    weight = np.where(np.arange(half) == 0, 1.0, 2.0)
    inverse = np.stack([cos_part * weight, sin_part * weight], axis=1)
    inverse = inverse.reshape(width, 2, members, columns).transpose(2, 1, 3, 0)
    inverse = inverse.reshape(members, 2 * columns, width)
    return forward, inverse


def column_table(quarter, sign):
    n = np.arange(quarter)
    angle = (n[:, None] * n[None, :] % quarter) * (2.0 * math.pi / quarter)
    c, s = np.cos(angle), sign * np.sin(angle)
    return np.block([[c, -s], [s, c]]).astype(np.float32)


def twist_table(height):
    quarter = height // 4
    angle = np.arange(4)[:, None] * np.arange(quarter)[None, :] * (2.0 * math.pi / height)
    return (
        np.cos(angle).astype(np.float32)[:, :, None],
        np.sin(angle).astype(np.float32)[:, :, None],
    )


def split(a, b):
    return jnp.einsum("ab,rbc->rac", a, b, precision=HIGH)


def mirrored(vec):
    flipped = vec[:, ::-1]
    return jnp.stack([jnp.roll(flipped[0], 1), flipped[3], flipped[2], flipped[1]])


def cross(nr, ni, fr, fi, scale):
    pr = nr * fr + ni * fi
    pi = ni * fr - nr * fi
    weight = 1.0 / (jnp.sqrt(pr * pr + pi * pi) + scale)
    return pr * weight, pi * weight


def rotate(ar, ai, br, bi):
    return ar * br - ai * bi, ar * bi + ai * br


def shards(right_face, left_face, intersection_list, slice_ranges):
    right = right_face[0]
    left = left_face[0]
    depth, rows, width = right.shape
    count = lax.axis_size("pencil")
    members = count // 2
    height = rows * count
    quarter = height // 4
    columns = width // (2 * members)
    scale = REG * height * width
    place = lax.axis_index("pencil")
    group = place // members
    member = place % members
    sign = (1 - 2 * group).astype(jnp.float32)

    live_count = intersection_list[0, 0]
    far_start = shift_tile(slice_ranges[:, 1:2], 1)[0, 0]

    def pick(slices, start, step):
        return lax.dynamic_index_in_dim(
            slices, jnp.minimum(start + step, depth - 1), 0, keepdims=False
        )

    near_start = slice_ranges[0, 0]
    right_keep = pick(right, near_start, group)
    right_send = pick(right, near_start, 1 - group)
    left_keep = pick(left, far_start, group)
    left_send = pick(left, far_start, 1 - group)
    left_got = swap_groups(left_send, members)
    far_own = shift_tile(left_keep, -1)
    right_got = swap_groups(right_send, members)
    far_other = shift_tile(left_got, -1)

    forward_np, inverse_np = row_tables(width, members)
    forward_hi, forward_lo = hi_lo(forward_np)
    table_hi = lax.dynamic_index_in_dim(forward_hi, member, 0, keepdims=False)
    table_lo = lax.dynamic_index_in_dim(forward_lo, member, 0, keepdims=False)

    def gathered(block):
        parts = [block] + [shift_members(block, members, s) for s in range(1, members)]
        if members == 2:
            first = member == 0
            ordered = [jnp.where(first, parts[0], parts[1]), jnp.where(first, parts[1], parts[0])]
            return jnp.concatenate(ordered, axis=0)
        order = (member - jnp.arange(members)) % members
        return jnp.take(jnp.stack(parts), order, axis=0).reshape(members * rows, width)

    def row_pass(block):
        pixels = gathered(block)
        spec = jnp.dot(pixels, table_hi, preferred_element_type=jnp.float32) + jnp.dot(
            pixels, table_lo, preferred_element_type=jnp.float32
        )
        return spec.reshape(2, quarter, 2 * columns)

    twist_cos, twist_sin = twist_table(height)
    forward_table = column_table(quarter, -1.0)

    def column_pass(own, other):
        even = own + other
        odd = (own - other) * sign
        er, ei = even[..., :columns], even[..., columns:]
        dr, di = odd[..., :columns], odd[..., columns:]
        zr = jnp.stack([er[0] + er[1], dr[0] + di[1], er[0] - er[1], dr[0] - di[1]])
        zi = jnp.stack([ei[0] + ei[1], di[0] - dr[1], ei[0] - ei[1], di[0] + dr[1]])
        zr, zi = rotate(zr, zi, twist_cos, -twist_sin)
        return split(forward_table, jnp.concatenate([zr, zi], axis=1))

    near = column_pass(row_pass(right_keep), row_pass(right_got))
    far = column_pass(row_pass(far_own), row_pass(far_other))
    nr, ni = near[:, :quarter], near[:, quarter:]
    fr, fi = far[:, :quarter], far[:, quarter:]

    factor = jnp.where(group < live_count, 1.0 / live_count.astype(jnp.float32), 0.0) * (
        1.0 / math.sqrt(height * width)
    )
    k = 4 * jnp.arange(quarter, dtype=jnp.int32)[None, :] + jnp.arange(4, dtype=jnp.int32)[:, None]
    angle_k = (k * intersection_list[0, 1] % height).astype(jnp.float32) * (2.0 * math.pi / height)
    kr, ki = jnp.cos(angle_k) * factor, jnp.sin(angle_k) * factor
    l = member * columns + jnp.arange(columns, dtype=jnp.int32)
    angle_l = (l * intersection_list[0, 2] % width).astype(jnp.float32) * (2.0 * math.pi / width)
    lr, li = jnp.cos(angle_l), jnp.sin(angle_l)

    pr, pi = cross(nr, ni, fr, fi, scale)
    pr, pi = rotate(pr, pi, kr[:, :, None], ki[:, :, None])
    pr, pi = rotate(pr, pi, lr, li)

    def unpack(vr, vi):
        mr, mi = mirrored(vr), mirrored(vi)
        return (
            0.5 * (vr + mr),
            0.5 * (vi - mi),
            0.5 * (vi + mi),
            0.5 * (mr - vr),
        )

    n0r, n0i, n1r, n1i = unpack(nr[:, :, 0], ni[:, :, 0])
    f0r, f0i, f1r, f1i = unpack(fr[:, :, 0], fi[:, :, 0])
    p0r, p0i = rotate(*cross(n0r, n0i, f0r, f0i, scale), kr, ki)
    p1r, p1i = rotate(*cross(n1r, n1i, f1r, f1i, scale), kr, ki)
    nyquist = (1 - 2 * ((width // 2 * intersection_list[0, 2] % width) // (width // 2))).astype(
        jnp.float32
    )
    packed_r = p0r - p1i * nyquist
    packed_i = p0i + p1r * nyquist
    first_column = jnp.logical_and(jnp.arange(columns) == 0, member == 0)
    pr = jnp.where(first_column, packed_r[:, :, None], pr)
    pi = jnp.where(first_column, packed_i[:, :, None], pi)

    waves = split(column_table(quarter, 1.0), jnp.concatenate([pr, pi], axis=1))
    ur, ui = rotate(waves[:, :quarter], waves[:, quarter:], twist_cos, twist_sin)
    even = jnp.stack(
        [
            jnp.concatenate([ur[0] + ur[2], ui[0] + ui[2]], axis=-1),
            jnp.concatenate([ur[0] - ur[2], ui[0] - ui[2]], axis=-1),
        ]
    )
    odd = sign * jnp.stack(
        [
            jnp.concatenate([ur[1] + ur[3], ui[1] + ui[3]], axis=-1),
            jnp.concatenate([ui[3] - ui[1], ur[1] - ur[3]], axis=-1),
        ]
    )
    own = (even + odd).reshape(members, rows, 2 * columns)
    other = (even - odd).reshape(members, rows, 2 * columns)

    inverse_table = jnp.asarray(inverse_np.astype(np.float32))
    own_parts, other_parts = [], []
    step = rows // CHUNKS
    for c in range(CHUNKS):
        cut = slice(c * step, (c + 1) * step)
        total = own[:, cut] + swap_groups(other[:, cut], members)
        result = None
        for s in range(members):
            target = (member + s) % members
            block = lax.dynamic_index_in_dim(total, target, 0, keepdims=False)
            if s > 0:
                block = shift_members(block, members, s)
            table = lax.dynamic_index_in_dim(
                inverse_table, (member - s) % members, 0, keepdims=False
            )
            term = jnp.dot(block, table, precision=HIGH)
            result = term if result is None else result + term
        own_parts.append(result)
        other_parts.append(shift_tile(result, 1))
    return jnp.stack([jnp.concatenate(own_parts), jnp.concatenate(other_parts)])[None]


def solution(mesh):
    faces = P(("blocks", "tile"), None, "pencil", None)
    lists = P(("blocks", "tile"), None)
    return jax.shard_map(
        shards,
        mesh=mesh,
        in_specs=(faces, faces, lists, lists),
        out_specs=faces,
        check_vma=False,
    )
```

time: 1420 us -> 583 us (0.41)
  waiting for transfers between devices: 666 us -> 250 us
  local copies, waits for them, and re-layouts: 233 us -> 89.2 us
  blocking collectives: 95.9 us -> 0 us
  other arithmetic: 164 us -> 74.9 us
  matrix products: 230 us -> 143 us
    all_to_all x2 -> x0, waiting for transfers between devices: 265 us -> none  [spectrum(): lax.all_to_all(row_spec, 'pencil', split_axis=3, concat_axis=2, tiled=True)]
    ppermute x2 -> x15, waiting for transfers between devices: 402 us -> 250 us  [the longest x4 155 us: swap_groups(): lax.ppermute(value, 'pencil', [(s, (s + members) % count) for s in range(...]
    all_to_all x1 -> x0, blocking collectives: 95.9 us -> none  [shards(): lax.all_to_all(col_spec, 'pencil', split_axis=1, concat_axis=2, tiled=True)]
    dot_general x12 -> x15, matrix products: 230 us -> 143 us  [the longest x3 54.4 us: split(): return jnp.einsum('ab,rbc->rac', a, b, precision=HIGH)]
    all_to_all x6 -> x0, local copies, waits for them, and re-layouts: 81.5 us -> none  [the longest x4 66.7 us: spectrum(): lax.all_to_all(row_spec, 'pencil', split_axis=3, concat_axis=2, tiled=True)]
    reshape x3 -> x0, local copies, waits for them, and re-layouts: 69.3 us -> none  [the longest x2 57.4 us: forward_dft(): return values.reshape((2,) + tail)]
    sub x7 -> x3, other arithmetic: 63.6 us -> 4.69 us  [rotate(): return (ar * br - ai * bi, ar * bi + ai * br)]
    gather x8 -> x0, local copies, waits for them, and re-layouts: 43.5 us -> none  [the longest x5 32.9 us: shards(): jnp.take(moved_spectra, jnp.minimum(start_far + slice_steps, depth - 1),...]
  transfers between devices with their start and end apart: 4 -> 15, of which waited for: 4 -> 7; matrix products, arithmetic and copies ran while one was open for 11% -> 23% of each run, Pallas kernels for 0% -> 0%
where the time goes in v1:
time: 583 us; the launch traced here: 577 us
  waiting for transfers between devices  250 us (43%)
  matrix products  143 us (25%)
  local copies, waits for them, and re-layouts  89.2 us (15%)
  other arithmetic  74.9 us (13%)
  starting transfers between devices  14.3 us (2%)
    ppermute x4, waiting for transfers between devices, swap_groups(): lax.ppermute(value, 'pencil', [(s, (s + members) % count) for s in range(...  155 us
    ppermute x5, waiting for transfers between devices, shift_tile(): lax.ppermute(value, 'tile', [(s, (s + steps) % count) for s in range(coun...  93.9 us
    dot_general x3, matrix products, split(): return jnp.einsum('ab,rbc->rac', a, b, precision=HIGH)  54.4 us
    dot_general x4, matrix products, row_pass(): jnp.dot(pixels, table_hi, preferred_element_type=jnp.float32)  34.6 us
    unnamed x88, local copies, waits for them, and re-layouts  32 us
    dot_general x4, matrix products, row_pass(): jnp.dot(pixels, table_lo, preferred_element_type=jnp.float32)  29.9 us
    dot_general x2, local copies, waits for them, and re-layouts, split(): return jnp.einsum('ab,rbc->rac', a, b, precision=HIGH)  24.2 us
    dot_general x4, matrix products, shards(): term = jnp.dot(block, table, precision=HIGH)  23.6 us
  transfers between devices with their start and end apart: 15, of which 7 were waited for; matrix products, arithmetic and copies ran while one was open for 23% of the time, Pallas kernels for 0%

profile of v1, /device:TPU:0, one launch (start us, length us, event | category | flops | bytes accessed | tf_op | source)
XLA Modules:
  0.0 576.7 jit_solution(5995354632115279095)
XLA Ops:
  2.6 4.0 dynamic-slice_bitcast_fusion.3
  6.6 3.0 collective-permute-start.1
  9.6 1.6 collective-permute-start.3
  18.2 2.7 dynamic-slice_bitcast_fusion.1
  20.9 2.3 collective-permute-start.4
  23.5 32.9 %collective-permute-done.1 = bf16[512,2048]{1,0:T(8,128)(2,1)} collective-permute-done((bf16[512,2048]{1,0:T(8,128)(2,1)}, bf16[512,2048]{1,0:T(8,128)(2,1)}, u32[]{:S(2)}, u32[]{:S(2)}) %collective-permute-start.1) | collective-permute-done | bytes 2097184 | tf_op jit(solution)/shard_map/ppermute | solution.py:22
  56.4 2.0 broadcast_select_fusion.7
  58.5 4.5 fusion.28
  63.0 6.1 %fusion.40 = f32[1024,1024]{1,0:T(8,128)} fusion(bf16[2,2048,1024]{2,1,0:T(8,128)(2,1)S(1)} %bitcast.209, s32[]{:T(128)S(6)} %select_n.163, bf16[512,2048]{1,0:T(8,128)(2,1)S(1)} %get-tuple-element.64, bf16[512,2048]{1,0:T(8,128)(2,1)S(1)} %get-tuple-element.63), kind=kOutput, calls=%fused_computation.56 | convolution fusion | flops 4303355904 | bytes 12582916 | tf_op jit(solution)/shard_map/dot_general | solution.py:143
  69.6 30.9 %collective-permute-done.6 = bf16[512,2048]{1,0:T(8,128)(2,1)} collective-permute-done((bf16[512,2048]{1,0:T(8,128)(2,1)S(1)}, bf16[512,2048]{1,0:T(8,128)(2,1)}, u32[]{:S(2)}, u32[]{:S(2)}) %collective-permute-start.6) | collective-permute-done | bytes 2097184 | tf_op jit(solution)/shard_map/ppermute | solution.py:22
  100.5 4.0 collective-permute-start.7
  104.5 1.9 broadcast_select_fusion.5
  106.4 9.4 %fusion.26 = f32[1024,1024]{1,0:T(8,128)} fusion(bf16[2,2048,1024]{2,1,0:T(8,128)(2,1)} %constant.170.clone, s32[]{:T(128)S(6)} %select_n.163, bf16[512,2048]{1,0:T(8,128)(2,1)S(1)} %get-tuple-element.68, bf16[512,2048]{1,0:T(8,128)(2,1)S(1)} %get-tuple-element.67), kind=kOutput, calls=%fused_computation.42 | convolution fusion | flops 4303355904 | bytes 12582916 | tf_op jit(solution)/shard_map/dot_general | solution.py:143
  115.7 11.3 %add_add_fusion.1 = (f32[1024,1024]{1,0:T(8,128)S(1)}, f32[1024,1024]{1,0:T(8,128)}) fusion(f32[1024,1024]{1,0:T(8,128)} %fusion.26, f32[1024,1024]{1,0:T(8,128)} %fusion.40, f32[1024,1024]{1,0:T(8,128)S(1)} %fusion.28, f32[]{:T(128)S(6)} %convert_element_type.39, bf16[2,2048,1024]{2,1,0:T(8,128)(2,1)} %constant.169.clone, s32[]{:T(128)S(6)} %select_n.163, ...), kind=kOutput, calls=%fused_computation.101 | convolution fusion | flops 4308598784 | bytes 29360136 | tf_op jit(solution)/shard_map/dot_general | solution.py:143
  127.0 1.8 fusion.96
  129.5 3.8 fusion.97
  133.4 2.5 copy.52
  137.2 1.6 copy.54
  138.8 2.5 copy.55
  141.3 2.5 copy.56
  143.8 2.6 copy.57
  146.4 2.5 fusion.100
  149.7 1.6 multiply_subtract_fusion.4
  151.9 16.4 %fusion = f32[4,512,1024]{2,1,0:T(8,128)} fusion(f32[1024,1024,1]{1,0,2:T(8,128)S(1)} %copy-done.20, f32[4,512,512]{1,2,0:T(8,128)S(1)} %get-tuple-element.22, f32[4,512,512]{1,2,0:T(8,128)S(1)} %get-tuple-element.21), kind=kOutput, calls=%fused_computation | convolution fusion | flops 12886999040 | bytes 20971520 | tf_op jit(solution)/shard_map/ab,rbc->rac/dot_general | solution.py:75
  168.3 12.1 %copy.73 = f32[4,512,1024]{2,0,1:T(4,128)} copy(f32[4,512,1024]{2,1,0:T(8,128)} %fusion) | data formatting | bytes 16777216 | tf_op jit(solution)/shard_map/ab,rbc->rac/dot_general | solution.py:75
  187.0 2.6 broadcast_select_fusion.3
  189.7 6.4 %fusion.24 = f32[1024,1024]{1,0:T(8,128)S(1)} fusion(bf16[2,2048,1024]{2,1,0:T(8,128)(2,1)} %constant.170.clone, s32[]{:T(128)S(6)} %select_n.163, bf16[512,2048]{1,0:T(8,128)(2,1)S(1)} %get-tuple-element.78, bf16[512,2048]{1,0:T(8,128)(2,1)S(1)} %get-tuple-element.77), kind=kOutput, calls=%fused_computation.40 | convolution fusion | flops 4303355904 | bytes 12582916 | tf_op jit(solution)/shard_map/dot_general | solution.py:143
  196.1 6.1 %fusion.36 = f32[1024,1024]{1,0:T(8,128)} fusion(bf16[2,2048,1024]{2,1,0:T(8,128)(2,1)S(1)} %bitcast.211, s32[]{:T(128)S(6)} %select_n.163, bf16[512,2048]{1,0:T(8,128)(2,1)S(1)} %get-tuple-element.78, bf16[512,2048]{1,0:T(8,128)(2,1)S(1)} %get-tuple-element.77), kind=kOutput, calls=%fused_computation.52 | convolution fusion | flops 4303355904 | bytes 12582916 | tf_op jit(solution)/shard_map/dot_general | solution.py:143
  202.2 1.9 broadcast_select_fusion.1
  204.1 9.5 %fusion.22 = f32[1024,1024]{1,0:T(8,128)} fusion(bf16[2,2048,1024]{2,1,0:T(8,128)(2,1)} %constant.170.clone, s32[]{:T(128)S(6)} %select_n.163, bf16[512,2048]{1,0:T(8,128)(2,1)S(1)} %get-tuple-element.82, bf16[512,2048]{1,0:T(8,128)(2,1)S(1)} %get-tuple-element.81), kind=kOutput, calls=%fused_computation.38 | convolution fusion | flops 4303355904 | bytes 12582916 | tf_op jit(solution)/shard_map/dot_general | solution.py:143
  213.6 11.1 %add_add_fusion = (f32[1024,1024]{1,0:T(8,128)S(1)}, f32[1024,1024]{1,0:T(8,128)}) fusion(f32[1024,1024]{1,0:T(8,128)} %fusion.22, f32[1024,1024]{1,0:T(8,128)} %fusion.36, f32[1024,1024]{1,0:T(8,128)S(1)} %fusion.24, f32[]{:T(128)S(6)} %convert_element_type.39, bf16[2,2048,1024]{2,1,0:T(8,128)(2,1)} %constant.169.clone, s32[]{:T(128)S(6)} %select_n.163, ...), kind=kOutput, calls=%fused_computation.100 | convolution fusion | flops 4308598784 | bytes 29360136 | tf_op jit(solution)/shard_map/dot_general | solution.py:143
  224.8 1.9 fusion.98
  227.3 3.9 fusion.99
  231.2 2.5 copy.60
  233.8 1.3 copy.61
  235.1 1.6 copy.62
  236.7 2.5 copy.63
  239.2 2.6 copy.64
  241.8 2.6 copy.65
  244.4 2.5 fusion.104
  247.4 1.6 multiply_subtract_fusion.3
  249.6 16.4 %fusion.4 = f32[4,512,1024]{2,1,0:T(8,128)} fusion(f32[1024,1024,1]{1,0,2:T(8,128)S(1)} %copy-done.21, f32[4,512,512]{1,2,0:T(8,128)S(1)} %get-tuple-element.24, f32[4,512,512]{1,2,0:T(8,128)S(1)} %get-tuple-element.23), kind=kOutput, calls=%fused_computation.4 | convolution fusion | flops 12886999040 | bytes 20971520 | tf_op jit(solution)/shard_map/ab,rbc->rac/dot_general | solution.py:75
  266.0 12.1 %copy.72 = f32[4,512,1024]{2,0,1:T(4,128)} copy(f32[4,512,1024]{2,1,0:T(8,128)} %fusion.4) | data formatting | bytes 16777216 | tf_op jit(solution)/shard_map/ab,rbc->rac/dot_general | solution.py:75
  280.3 9.6 %multiply_add_fusion.2 = (f32[4,512,512]{1,0,2:T(4,128)}, f32[4,512,512]{1,0,2:T(4,128)}) fusion(f32[4,1024,512]{1,0,2:T(4,128)} %bitcast.178, f32[4,1024,512]{1,0,2:T(4,128)} %bitcast.175), kind=kLoop, calls=%fused_computation.70 | loop fusion | flops 6291456 | bytes 25165824 | tf_op jit(solution)/shard_map/add | solution.py:84
  294.2 1.5 subtract_bitcast_fusion.4
  296.4 11.0 %subtract_select_fusion = (f32[4,512,512]{1,0,2:T(4,128)}, f32[4,512,512]{1,0,2:T(4,128)S(1)}, f32[4,512,512]{1,0,2:T(4,128)S(1)}) fusion(f32[512]{0:T(512)S(1)} %copy-done.15, f32[512]{0:T(512)S(1)} %copy-done.16, f32[4,512]{1,0:T(4,128)S(1)} %get-tuple-element.8, pred[512]{0:T(512)(128)(4,1)S(1)} %copy-done.19, f32[4,512]{1,0:T(4,128)S(1)} %copy-done.12, ...), kind=kLoop, calls=%fused_computation.65 | loop fusion | flops 17825792 | bytes 21000704 | tf_op jit(solution)/shard_map/jit(_where)/select_n | solution.py:199
  307.4 4.4 add_select_fusion
  311.9 9.1 %pad_maximum_fusion = f32[4,1024,512]{1,0,2:T(4,128)} fusion(f32[4,512,512]{1,0,2:T(4,128)} %add_select_fusion, f32[4,512,512]{1,0,2:T(4,128)} %get-tuple-element.5), kind=kLoop, calls=%fused_computation.8 | loop fusion | flops 2097152 | bytes 16777216 | tf_op jit(solution)/shard_map/concatenate | solution.py:202
  321.0 21.6 %fusion.48 = f32[4,1024,512]{1,2,0:T(8,128)S(1)} fusion(f32[1024,1024,1]{1,0,2:T(8,128)} %constant.185, f32[4,1024,512]{1,0,2:T(4,128)} %pad_maximum_fusion), kind=kOutput, calls=%fused_computation.79 | convolution fusion | flops 12884901888 | bytes 20971520 | tf_op jit(solution)/shard_map/ab,rbc->rac/dot_general | solution.py:75
  342.6 1.5 multiply_subtract_fusion
  345.9 3.1 fusion.47
  349.0 2.3 fusion.95
  351.2 1.5 collective-permute-start.11
  353.3 46.6 %collective-permute-done.11 = f32[2,256,1024]{1,2,0:T(8,128)S(1)} collective-permute-done((f32[2,256,1024]{1,2,0:T(8,128)}, f32[2,256,1024]{1,2,0:T(8,128)S(1)}, u32[]{:S(2)}, u32[]{:S(2)}) %collective-permute-start.11) | collective-permute-done | bytes 2097184 | tf_op jit(solution)/shard_map/ppermute | solution.py:22
  399.9 44.6 %collective-permute-done.9 = f32[2,256,1024]{1,2,0:T(8,128)} collective-permute-done((f32[2,256,1024]{1,2,0:T(8,128)}, f32[2,256,1024]{1,2,0:T(8,128)}, u32[]{:S(2)}, u32[]{:S(2)}) %collective-permute-start.9) | collective-permute-done | bytes 2097184 | tf_op jit(solution)/shard_map/ppermute | solution.py:22
  444.5 4.1 slice_add_fusion.1
  452.6 1.5 collective-permute-done.10
  454.0 6.6 %fusion.10 = f32[256,2048]{1,0:T(8,128)S(1)} fusion(f32[256,1024]{0,1:T(8,128)} %collective-permute-done.10, f32[2,1024,2048]{2,1,0:T(8,128)} %constant.176.clone, s32[]{:T(128)S(6)} %select_n.186), kind=kOutput, calls=%fused_computation.12 | convolution fusion | flops 3221225472 | bytes 11534340 | tf_op jit(solution)/shard_map/dot_general | solution.py:234
  460.6 6.6 %fusion.51 = f32[256,2048]{1,0:T(8,128)S(1)} fusion(f32[256,2048]{1,0:T(8,128)S(1)} %fusion.10, f32[2,1024,2048]{2,1,0:T(8,128)} %constant.176.clone, s32[]{:T(128)S(6)} %select_n.182, f32[2,256,1024]{1,2,0:T(8,128)S(1)} %copy-done.1), kind=kOutput, calls=%fused_computation.80 | convolution fusion | flops 3221749760 | bytes 13632512 | tf_op jit(solution)/shard_map/dot_general | solution.py:234
  467.2 6.3 %fusion.8 = f32[256,2048]{1,0:T(8,128)S(1)} fusion(f32[256,1024]{0,1:T(8,128)S(1)} %collective-permute-done.12, f32[2,1024,2048]{2,1,0:T(8,128)} %constant.176.clone, s32[]{:T(128)S(6)} %select_n.186), kind=kOutput, calls=%fused_computation.10 | convolution fusion | flops 3221225472 | bytes 11534340 | tf_op jit(solution)/shard_map/dot_general | solution.py:234
  473.6 4.2 fusion.54
  478.4 49.7 %collective-permute-done.13 = f32[256,2048]{1,0:T(8,128)S(1)} collective-permute-done((f32[256,2048]{1,0:T(8,128)S(1)}, f32[256,2048]{1,0:T(8,128)S(1)}, u32[]{:S(2)}, u32[]{:S(2)}) %collective-permute-start.13) | collective-permute-done | bytes 2097184 | tf_op jit(solution)/shard_map/ppermute | solution.py:17
  528.1 44.1 %collective-permute-done.14 = f32[256,2048]{1,0:T(8,128)S(1)} collective-permute-done((f32[256,2048]{1,0:T(8,128)S(1)}, f32[256,2048]{1,0:T(8,128)S(1)}, u32[]{:S(2)}, u32[]{:S(2)}) %collective-permute-start.14) | collective-permute-done | bytes 2097184 | tf_op jit(solution)/shard_map/ppermute | solution.py:17
  572.5 4.0 maximum_bitcast_fusion
  (144 shorter events, 31.7 us)
Async XLA Ops:
  2.6 8.6 %copy-start.18 = (s32[1,3]{1,0:T(1,128)S(1)}, s32[1,3]{1,0:T(1,128)}, u32[]{:S(2)}) copy-start(s32[1,3]{1,0:T(1,128)} %param.16) | copy-start | bytes 40
  6.6 49.7 %collective-permute-start.1 = (bf16[512,2048]{1,0:T(8,128)(2,1)}, bf16[512,2048]{1,0:T(8,128)(2,1)}, u32[]{:S(2)}, u32[]{:S(2)}) collective-permute-start(bf16[512,2048]{1,0:T(8,128)(2,1)} %get-tuple-element.66), channel_id=1, source_target_pairs={{0,8},{4,12},{8,0},{12,4},{1,9},{5,13},{9,1},{13,5},{2,10},{6,14},... | collective-permute-start | bytes 6291464 | tf_op jit(solution)/shard_map/ppermute | solution.py:22
  9.6 46.8 %collective-permute-start = (bf16[512,2048]{1,0:T(8,128)(2,1)S(1)}, bf16[512,2048]{1,0:T(8,128)(2,1)}, u32[]{:S(2)}, u32[]{:S(2)}) collective-permute-start(bf16[512,2048]{1,0:T(8,128)(2,1)S(1)} %get-tuple-element.65), channel_id=1, source_target_pairs={{0,4},{4,0},{8,12},{12,8},{1,5},{5,1},{9,13},{13,9},{2,6},{6,2},{1... | collective-permute-start | bytes 6291464 | tf_op jit(solution)/shard_map/ppermute | solution.py:31
  9.6 7.3 %collective-permute-start.3 = (s32[1,1]{1,0:T(1,128)}, s32[1,1]{1,0:T(1,128)}, u32[]{:S(2)}, u32[]{:S(2)}) collective-permute-start(s32[1,1]{1,0:T(1,128)} %get-tuple-element.102), channel_id=1, source_target_pairs={{0,1},{1,2},{2,3},{3,0},{4,5},{5,6},{6,7},{7,4},{8,9},{9,10},{10,1... | collective-permute-start | bytes 20 | tf_op jit(solution)/shard_map/ppermute | solution.py:17
  14.4 1.3 copy-start.13
  18.2 40.3 %slice-start.8 = ((s8[8388608]{0:T(1024)(128)(4,1)}), s8[4194304]{0:T(1024)(128)(4,1)S(1)}, s32[]{:S(2)}) async-start(s8[8388608]{0:T(1024)(128)(4,1)} %bitcast.212), calls=%async_computation.8 | async-start | bytes 8388608
  20.9 37.6 %slice-start.9 = ((s8[8388608]{0:T(1024)(128)(4,1)}), s8[4194304]{0:T(1024)(128)(4,1)S(1)}, s32[]{:S(2)}) async-start(s8[8388608]{0:T(1024)(128)(4,1)} %bitcast.212), calls=%async_computation.9 | async-start | bytes 8388608
  20.9 48.2 %collective-permute-start.4 = (bf16[512,2048]{1,0:T(8,128)(2,1)S(1)}, bf16[512,2048]{1,0:T(8,128)(2,1)}, u32[]{:S(2)}, u32[]{:S(2)}) collective-permute-start(bf16[512,2048]{1,0:T(8,128)(2,1)S(1)} %get-tuple-element.79), channel_id=1, source_target_pairs={{0,3},{1,0},{2,1},{3,2},{4,7},{5,4},{6,5},{7,6},{8,11},{9,8},{10,9... | collective-permute-start | bytes 6291464 | tf_op jit(solution)/shard_map/ppermute | solution.py:17
  23.2 77.3 %collective-permute-start.6 = (bf16[512,2048]{1,0:T(8,128)(2,1)S(1)}, bf16[512,2048]{1,0:T(8,128)(2,1)}, u32[]{:S(2)}, u32[]{:S(2)}) collective-permute-start(bf16[512,2048]{1,0:T(8,128)(2,1)S(1)} %get-tuple-element.80), channel_id=1, source_target_pairs={{0,8},{4,12},{8,0},{12,4},{1,9},{5,13},{9,1},{13,5},{2,10},{6,14},... | collective-permute-start | bytes 6291464 | tf_op jit(solution)/shard_map/ppermute | solution.py:22
  56.4 48.1 %collective-permute-start.2 = (bf16[512,2048]{1,0:T(8,128)(2,1)}, bf16[512,2048]{1,0:T(8,128)(2,1)S(1)}, u32[]{:S(2)}, u32[]{:S(2)}) collective-permute-start(bf16[512,2048]{1,0:T(8,128)(2,1)} %collective-permute-done.1), channel_id=1, source_target_pairs={{0,4},{4,0},{8,12},{12,8},{1,5},{5,1},{9,13},{13,9},{2,6},{6,2},{1... | collective-permute-start | bytes 6291464 | tf_op jit(solution)/shard_map/ppermute | solution.py:31
  56.4 6.6 %slice-start.4 = ((s8[8388608]{0:T(1024)(128)(4,1)}), s8[4194304]{0:T(1024)(128)(4,1)S(1)}, s32[]{:S(2)}) async-start(s8[8388608]{0:T(1024)(128)(4,1)} %bitcast.208), calls=%async_computation.4 | async-start | bytes 8388608
  58.4 4.5 slice-start.5
  69.1 117.9 %collective-permute-start.5 = (bf16[512,2048]{1,0:T(8,128)(2,1)}, bf16[512,2048]{1,0:T(8,128)(2,1)}, u32[]{:S(2)}, u32[]{:S(2)}) collective-permute-start(bf16[512,2048]{1,0:T(8,128)(2,1)} %collective-permute-done.4), channel_id=1, source_target_pairs={{0,4},{4,0},{8,12},{12,8},{1,5},{5,1},{9,13},{13,9},{2,6},{6,2},{1... | collective-permute-start | bytes 6291464 | tf_op jit(solution)/shard_map/ppermute | solution.py:31
  100.5 86.4 %collective-permute-start.7 = (bf16[512,2048]{1,0:T(8,128)(2,1)}, bf16[512,2048]{1,0:T(8,128)(2,1)}, u32[]{:S(2)}, u32[]{:S(2)}) collective-permute-start(bf16[512,2048]{1,0:T(8,128)(2,1)} %collective-permute-done.6), channel_id=1, source_target_pairs={{0,3},{1,0},{2,1},{3,2},{4,7},{5,4},{6,5},{7,6},{8,11},{9,8},{10,9... | collective-permute-start | bytes 6291464 | tf_op jit(solution)/shard_map/ppermute | solution.py:17
  146.4 2.5 copy-start.2
  146.4 2.5 copy-start.4
  146.4 2.6 copy-start.6
  149.0 0.7 copy-start.9
  149.0 0.7 copy-start.10
  149.7 2.2 copy-start.20
  187.0 15.3 %collective-permute-start.8 = (bf16[512,2048]{1,0:T(8,128)(2,1)}, bf16[512,2048]{1,0:T(8,128)(2,1)S(1)}, u32[]{:S(2)}, u32[]{:S(2)}) collective-permute-start(bf16[512,2048]{1,0:T(8,128)(2,1)} %collective-permute-done.7), channel_id=1, source_target_pairs={{0,4},{4,0},{8,12},{12,8},{1,5},{5,1},{9,13},{13,9},{2,6},{6,2},{1... | collective-permute-start | bytes 6291464 | tf_op jit(solution)/shard_map/ppermute | solution.py:31
  187.0 9.1 %slice-start.6 = ((s8[8388608]{0:T(1024)(128)(4,1)}), s8[4194304]{0:T(1024)(128)(4,1)S(1)}, s32[]{:S(2)}) async-start(s8[8388608]{0:T(1024)(128)(4,1)} %bitcast.210), calls=%async_computation.6 | async-start | bytes 8388608
  189.7 6.5 %slice-start.7 = ((s8[8388608]{0:T(1024)(128)(4,1)}), s8[4194304]{0:T(1024)(128)(4,1)S(1)}, s32[]{:S(2)}) async-start(s8[8388608]{0:T(1024)(128)(4,1)} %bitcast.210), calls=%async_computation.7 | async-start | bytes 8388608
  244.4 2.5 copy-start.3
  244.4 2.5 copy-start.5
  244.4 2.6 copy-start.7
  247.4 2.2 copy-start.21
  280.2 14.0 %copy-start.14 = (s32[512]{0:T(512)S(1)}, s32[512]{0:T(512)}, u32[]{:S(2)}) copy-start(s32[512]{0:T(512)} %copy-done.13) | copy-start | bytes 6148
  280.2 16.1 %copy-start.11 = (f32[4,512]{1,0:T(4,128)S(1)}, f32[4,512]{1,0:T(4,128)}, u32[]{:S(2)}) copy-start(f32[4,512]{1,0:T(4,128)} %get-tuple-element.99) | copy-start | bytes 24580
  280.2 16.1 %copy-start.12 = (f32[4,512]{1,0:T(4,128)S(1)}, f32[4,512]{1,0:T(4,128)}, u32[]{:S(2)}) copy-start(f32[4,512]{1,0:T(4,128)} %get-tuple-element.100) | copy-start | bytes 24580
  280.3 16.1 %copy-start.15 = (f32[512]{0:T(512)S(1)}, f32[512]{0:T(512)}, u32[]{:S(2)}) copy-start(f32[512]{0:T(512)} %get-tuple-element.106) | copy-start | bytes 6148
  280.3 16.1 %copy-start.16 = (f32[512]{0:T(512)S(1)}, f32[512]{0:T(512)}, u32[]{:S(2)}) copy-start(f32[512]{0:T(512)} %get-tuple-element.107) | copy-start | bytes 6148
  280.3 16.1 %copy-start.19 = (pred[512]{0:T(512)(128)(4,1)S(1)}, pred[512]{0:T(512)(128)(4,1)}, u32[]{:S(2)}) copy-start(pred[512]{0:T(512)(128)(4,1)} %fusion.82) | copy-start | bytes 1540
  321.0 21.6 %copy-start.17 = (f32[4,512]{1,0:T(4,128)S(1)}, f32[4,512]{1,0:T(4,128)}, u32[]{:S(2)}) copy-start(f32[4,512]{1,0:T(4,128)} %constant.183) | copy-start | bytes 24580
  351.2 48.6 %collective-permute-start.11 = (f32[2,256,1024]{1,2,0:T(8,128)}, f32[2,256,1024]{1,2,0:T(8,128)S(1)}, u32[]{:S(2)}, u32[]{:S(2)}) collective-permute-start(f32[2,256,1024]{1,2,0:T(8,128)} %get-tuple-element.46), channel_id=1, source_target_pairs={{0,8},{4,12},{8,0},{12,4},{1,9},{5,13},{9,1},{13,5},{2,10},{6,14},... | collective-permute-start | bytes 6291464 | tf_op jit(solution)/shard_map/ppermute | solution.py:22
  352.7 91.8 %collective-permute-start.9 = (f32[2,256,1024]{1,2,0:T(8,128)}, f32[2,256,1024]{1,2,0:T(8,128)}, u32[]{:S(2)}, u32[]{:S(2)}) collective-permute-start(f32[2,256,1024]{1,2,0:T(8,128)} %get-tuple-element.45), channel_id=1, source_target_pairs={{0,8},{4,12},{8,0},{12,4},{1,9},{5,13},{9,1},{13,5},{2,10},{6,14},... | collective-permute-start | bytes 6291464 | tf_op jit(solution)/shard_map/ppermute | solution.py:22
  399.9 44.6 %copy-start.8 = (f32[2,256,1024]{1,2,0:T(8,128)}, f32[2,256,1024]{1,2,0:T(8,128)S(1)}, u32[]{:S(2)}) copy-start(f32[2,256,1024]{1,2,0:T(8,128)S(1)} %collective-permute-done.11) | copy-start | bytes 6291460
  448.6 1.3 copy-start
  451.0 3.0 collective-permute-start.10
  452.0 15.2 %collective-permute-start.12 = (f32[256,1024]{0,1:T(8,128)}, f32[256,1024]{0,1:T(8,128)S(1)}, u32[]{:S(2)}, u32[]{:S(2)}) collective-permute-start(f32[256,1024]{0,1:T(8,128)} %dynamic-slice_bitcast_fusion.4), channel_id=1, source_target_pairs={{0,4},{4,0},{8,12},{12,8},{1,5},{5,1},{9,13},{13,9},{2,6},{6,2},{1... | collective-permute-start | bytes 3145736 | tf_op jit(solution)/shard_map/ppermute | solution.py:31
  452.6 8.0 %copy-start.1 = (f32[2,256,1024]{1,2,0:T(8,128)S(1)}, f32[2,256,1024]{1,2,0:T(8,128)}, u32[]{:S(2)}) copy-start(f32[2,256,1024]{1,2,0:T(8,128)} %copy-done) | copy-start | bytes 6291460
  454.0 19.5 %slice-start = ((s8[16777216]{0:T(1024)(128)(4,1)}), s8[4194304]{0:T(1024)(128)(4,1)S(1)}, s32[]{:S(2)}) async-start(s8[16777216]{0:T(1024)(128)(4,1)} %bitcast.172), calls=%async_computation | async-start | bytes 8388608
  454.0 19.5 %slice-start.1 = ((s8[16777216]{0:T(1024)(128)(4,1)}), s8[4194304]{0:T(1024)(128)(4,1)S(1)}, s32[]{:S(2)}) async-start(s8[16777216]{0:T(1024)(128)(4,1)} %bitcast.172), calls=%async_computation.1 | async-start | bytes 8388608
  460.6 13.0 %slice-start.2 = ((s8[16777216]{0:T(1024)(128)(4,1)}), s8[4194304]{0:T(1024)(128)(4,1)S(1)}, s32[]{:S(2)}) async-start(s8[16777216]{0:T(1024)(128)(4,1)} %bitcast.172), calls=%async_computation.2 | async-start | bytes 8388608
  467.2 6.3 %slice-start.3 = ((s8[16777216]{0:T(1024)(128)(4,1)}), s8[4194304]{0:T(1024)(128)(4,1)S(1)}, s32[]{:S(2)}) async-start(s8[16777216]{0:T(1024)(128)(4,1)} %bitcast.172), calls=%async_computation.3 | async-start | bytes 8388608
  477.8 50.3 %collective-permute-start.13 = (f32[256,2048]{1,0:T(8,128)S(1)}, f32[256,2048]{1,0:T(8,128)S(1)}, u32[]{:S(2)}, u32[]{:S(2)}) collective-permute-start(f32[256,2048]{1,0:T(8,128)S(1)} %fusion.51), channel_id=1, source_target_pairs={{0,1},{1,2},{2,3},{3,0},{4,5},{5,6},{6,7},{7,4},{8,9},{9,10},{10,1... | collective-permute-start | bytes 6291464 | tf_op jit(solution)/shard_map/ppermute | solution.py:17
  477.8 94.4 %collective-permute-start.14 = (f32[256,2048]{1,0:T(8,128)S(1)}, f32[256,2048]{1,0:T(8,128)S(1)}, u32[]{:S(2)}, u32[]{:S(2)}) collective-permute-start(f32[256,2048]{1,0:T(8,128)S(1)} %fusion.54), channel_id=1, source_target_pairs={{0,1},{1,2},{2,3},{3,0},{4,5},{5,6},{6,7},{7,4},{8,9},{9,10},{10,1... | collective-permute-start | bytes 6291464 | tf_op jit(solution)/shard_map/ppermute | solution.py:17

commit v2 on v1

--- a/solution.py
+++ b/solution.py
@@ -72,7 +72,23 @@
 
 
 def split(a, b):
-    return jnp.einsum("ab,rbc->rac", a, b, precision=HIGH)
+    return jnp.dot(a, b, precision=HIGH)
+
+
+def encode(value):
+    tall = value.shape[-2]
+    group = math.gcd(tall, 64)
+    grouped = value.reshape(value.shape[:-2] + (tall // group, group, value.shape[-1]))
+    peak = jnp.maximum(jnp.max(jnp.abs(grouped), axis=-2, keepdims=True), 1e-30)
+    coded = jnp.round(grouped * (32767.0 / peak)).astype(jnp.int16)
+    return coded.reshape(value.shape), jnp.squeeze(peak, axis=-2) * (1.0 / 32767.0)
+
+
+def decode(coded, scale):
+    tall = coded.shape[-2]
+    count = scale.shape[-2]
+    grouped = coded.reshape(coded.shape[:-2] + (count, tall // count, coded.shape[-1]))
+    return (grouped.astype(jnp.float32) * scale[..., None, :]).reshape(coded.shape)
 
 
 def mirrored(vec):
@@ -153,16 +169,21 @@
         odd = (own - other) * sign
         er, ei = even[..., :columns], even[..., columns:]
         dr, di = odd[..., :columns], odd[..., columns:]
-        zr = jnp.stack([er[0] + er[1], dr[0] + di[1], er[0] - er[1], dr[0] - di[1]])
-        zi = jnp.stack([ei[0] + ei[1], di[0] - dr[1], ei[0] - ei[1], di[0] + dr[1]])
-        zr, zi = rotate(zr, zi, twist_cos, -twist_sin)
-        return split(forward_table, jnp.concatenate([zr, zi], axis=1))
+        parts = [
+            (er[0] + er[1], ei[0] + ei[1]),
+            (dr[0] + di[1], di[0] - dr[1]),
+            (er[0] - er[1], ei[0] - ei[1]),
+            (dr[0] - di[1], di[0] + dr[1]),
+        ]
+        result = []
+        for r in range(4):
+            turned = rotate(*parts[r], twist_cos[r], -twist_sin[r])
+            spec = split(forward_table, jnp.concatenate(turned, axis=0))
+            result.append((spec[:quarter], spec[quarter:]))
+        return result
 
     near = column_pass(row_pass(right_keep), row_pass(right_got))
     far = column_pass(row_pass(far_own), row_pass(far_other))
-    nr, ni = near[:, :quarter], near[:, quarter:]
-    fr, fi = far[:, :quarter], far[:, quarter:]
-
     factor = jnp.where(group < live_count, 1.0 / live_count.astype(jnp.float32), 0.0) * (
         1.0 / math.sqrt(height * width)
     )
@@ -172,10 +193,6 @@
     l = member * columns + jnp.arange(columns, dtype=jnp.int32)
     angle_l = (l * intersection_list[0, 2] % width).astype(jnp.float32) * (2.0 * math.pi / width)
     lr, li = jnp.cos(angle_l), jnp.sin(angle_l)
-
-    pr, pi = cross(nr, ni, fr, fi, scale)
-    pr, pi = rotate(pr, pi, kr[:, :, None], ki[:, :, None])
-    pr, pi = rotate(pr, pi, lr, li)
 
     def unpack(vr, vi):
         mr, mi = mirrored(vr), mirrored(vi)
@@ -186,8 +203,11 @@
             0.5 * (mr - vr),
         )
 
-    n0r, n0i, n1r, n1i = unpack(nr[:, :, 0], ni[:, :, 0])
-    f0r, f0i, f1r, f1i = unpack(fr[:, :, 0], fi[:, :, 0])
+    def first(spec):
+        return unpack(jnp.stack([v[0][:, 0] for v in spec]), jnp.stack([v[1][:, 0] for v in spec]))
+
+    n0r, n0i, n1r, n1i = first(near)
+    f0r, f0i, f1r, f1i = first(far)
     p0r, p0i = rotate(*cross(n0r, n0i, f0r, f0i, scale), kr, ki)
     p1r, p1i = rotate(*cross(n1r, n1i, f1r, f1i, scale), kr, ki)
     nyquist = (1 - 2 * ((width // 2 * intersection_list[0, 2] % width) // (width // 2))).astype(
@@ -196,11 +216,18 @@
     packed_r = p0r - p1i * nyquist
     packed_i = p0i + p1r * nyquist
     first_column = jnp.logical_and(jnp.arange(columns) == 0, member == 0)
-    pr = jnp.where(first_column, packed_r[:, :, None], pr)
-    pi = jnp.where(first_column, packed_i[:, :, None], pi)
-
-    waves = split(column_table(quarter, 1.0), jnp.concatenate([pr, pi], axis=1))
-    ur, ui = rotate(waves[:, :quarter], waves[:, quarter:], twist_cos, twist_sin)
+    inverse_column = column_table(quarter, 1.0)
+    ur, ui = [], []
+    for r in range(4):
+        pr, pi = cross(*near[r], *far[r], scale)
+        pr, pi = rotate(pr, pi, kr[r][:, None], ki[r][:, None])
+        pr, pi = rotate(pr, pi, lr, li)
+        pr = jnp.where(first_column, packed_r[r][:, None], pr)
+        pi = jnp.where(first_column, packed_i[r][:, None], pi)
+        wave = split(inverse_column, jnp.concatenate([pr, pi], axis=0))
+        turned = rotate(wave[:quarter], wave[quarter:], twist_cos[r], twist_sin[r])
+        ur.append(turned[0])
+        ui.append(turned[1])
     even = jnp.stack(
         [
             jnp.concatenate([ur[0] + ur[2], ui[0] + ui[2]], axis=-1),
@@ -221,7 +248,11 @@
     step = rows // CHUNKS
     for c in range(CHUNKS):
         cut = slice(c * step, (c + 1) * step)
-        total = own[:, cut] + swap_groups(other[:, cut], members)
+        sent = encode(other[:, cut])
+        if c > 0:
+            sent, got = lax.optimization_barrier((sent, got))
+        got = tuple(swap_groups(v, members) for v in sent)
+        total = own[:, cut] + decode(*got)
         result = None
         for s in range(members):
             target = (member + s) % members
@@ -234,7 +265,7 @@
             term = jnp.dot(block, table, precision=HIGH)
             result = term if result is None else result + term
         own_parts.append(result)
-        other_parts.append(shift_tile(result, 1))
+        other_parts.append(decode(*[shift_tile(v, 1) for v in encode(result)]))
     return jnp.stack([jnp.concatenate(own_parts), jnp.concatenate(other_parts)])[None]
 
 

time: 583 us -> 490 us (0.84)
  waiting for transfers between devices: 250 us -> 151 us
  other arithmetic: 74.9 us -> 46 us
  matrix products: 143 us -> 162 us
  local copies, waits for them, and re-layouts: 89.2 us -> 103 us
  starting transfers between devices: 14.3 us -> 21.3 us
    ppermute x5 -> x7, waiting for transfers between devices: 93.9 us -> 40.6 us  [shift_tile(): lax.ppermute(value, 'tile', [(s, (s + steps) % count) for s in range(coun...]
    ppermute x4 -> x6, waiting for transfers between devices: 155 us -> 110 us  [swap_groups(): lax.ppermute(value, 'pencil', [(s, (s + members) % count) for s in range(...]
    unnamed x88 -> x182, local copies, waits for them, and re-layouts: 32 us -> 58.8 us
    dot_general x2 -> x0, local copies, waits for them, and re-layouts: 24.2 us -> none  [split(): return jnp.einsum('ab,rbc->rac', a, b, precision=HIGH)]
    dot_general x3 -> x24, matrix products: 54.4 us -> 73.3 us  [split(): return jnp.dot(a, b, precision=HIGH)]
    add x7 -> x3, other arithmetic: 22.8 us -> 5.98 us  [the longest x1 4.54 us: shards(): total = own[:, cut] + decode(*got)]
    select_n x2 -> x0, other arithmetic: 15.5 us -> none  [the longest x1 11 us: shards(): pr = jnp.where(first_column, packed_r[:, :, None], pr)]
    mul x0 -> x8, local copies, waits for them, and re-layouts: none -> 12.2 us  [the longest x4 8.07 us: encode(): coded = jnp.round(grouped * (32767.0 / peak)).astype(jnp.int16)]
  transfers between devices with their start and end apart: 15 -> 19, of which waited for: 7 -> 5; matrix products, arithmetic and copies ran while one was open for 23% -> 30% of each run, Pallas kernels for 0% -> 0%
where the time goes in v2:
time: 490 us; the launch traced here: 489 us
  matrix products  162 us (33%)
  waiting for transfers between devices  151 us (31%)
  local copies, waits for them, and re-layouts  103 us (21%)
  other arithmetic  46 us (9%)
  starting transfers between devices  21.3 us (4%)
  between operations  6.52 us (1%)
    ppermute x6, waiting for transfers between devices, swap_groups(): lax.ppermute(value, 'pencil', [(s, (s + members) % count) for s in range(...  110 us
    dot_general x24, matrix products, split(): return jnp.dot(a, b, precision=HIGH)  73.3 us
    unnamed x182, local copies, waits for them, and re-layouts  58.8 us
    ppermute x7, waiting for transfers between devices, shift_tile(): lax.ppermute(value, 'tile', [(s, (s + steps) % count) for s in range(coun...  40.6 us
    dot_general x4, matrix products, row_pass(): jnp.dot(pixels, table_hi, preferred_element_type=jnp.float32)  35.4 us
    dot_general x4, matrix products, row_pass(): jnp.dot(pixels, table_lo, preferred_element_type=jnp.float32)  29.7 us
    dot_general x4, matrix products, shards(): term = jnp.dot(block, table, precision=HIGH)  23.9 us
    ppermute x7, starting transfers between devices, shift_tile(): lax.ppermute(value, 'tile', [(s, (s + steps) % count) for s in range(coun...  12.9 us
  transfers between devices with their start and end apart: 19, of which 5 were waited for; matrix products, arithmetic and copies ran while one was open for 30% of the time, Pallas kernels for 0%

profile of v2, /device:TPU:0, one launch (start us, length us, event | category | flops | bytes accessed | tf_op | source)
XLA Modules:
  0.0 489.2 jit_solution(13586988903770196064)
XLA Ops:
  2.6 4.0 dynamic-slice_bitcast_fusion.3
  6.7 3.0 collective-permute-start.1
  17.6 2.7 dynamic-slice_bitcast_fusion.1
  20.3 2.3 collective-permute-start.4
  22.9 33.5 %collective-permute-done.1 = bf16[512,2048]{1,0:T(8,128)(2,1)} collective-permute-done((bf16[512,2048]{1,0:T(8,128)(2,1)}, bf16[512,2048]{1,0:T(8,128)(2,1)}, u32[]{:S(2)}, u32[]{:S(2)}) %collective-permute-start.1) | collective-permute-done | bytes 2097184 | tf_op jit(solution)/shard_map/ppermute | solution.py:22
  56.4 2.0 broadcast_select_fusion.7
  58.5 4.5 fusion.18
  63.0 6.1 %fusion.30 = f32[1024,1024]{1,0:T(8,128)} fusion(bf16[2,2048,1024]{2,1,0:T(8,128)(2,1)S(1)} %bitcast.410, s32[]{:T(128)S(6)} %select_n.164, bf16[512,2048]{1,0:T(8,128)(2,1)S(1)} %get-tuple-element.50, bf16[512,2048]{1,0:T(8,128)(2,1)S(1)} %get-tuple-element.49), kind=kOutput, calls=%fused_computation.39 | convolution fusion | flops 4303355904 | bytes 12582916 | tf_op jit(solution)/shard_map/dot_general | solution.py:159
  69.7 30.8 %collective-permute-done.6 = bf16[512,2048]{1,0:T(8,128)(2,1)} collective-permute-done((bf16[512,2048]{1,0:T(8,128)(2,1)S(1)}, bf16[512,2048]{1,0:T(8,128)(2,1)}, u32[]{:S(2)}, u32[]{:S(2)}) %collective-permute-start.6) | collective-permute-done | bytes 2097184 | tf_op jit(solution)/shard_map/ppermute | solution.py:22
  100.5 4.0 collective-permute-start.7
  106.4 9.4 %fusion.16 = f32[1024,1024]{1,0:T(8,128)} fusion(bf16[2,2048,1024]{2,1,0:T(8,128)(2,1)} %constant.199.clone, s32[]{:T(128)S(6)} %select_n.164, bf16[512,2048]{1,0:T(8,128)(2,1)S(1)} %get-tuple-element.54, bf16[512,2048]{1,0:T(8,128)(2,1)S(1)} %get-tuple-element.53), kind=kOutput, calls=%fused_computation.25 | convolution fusion | flops 4303355904 | bytes 12582916 | tf_op jit(solution)/shard_map/dot_general | solution.py:159
  115.7 11.6 %add_add_fusion.1 = (f32[1024,1024]{1,0:T(8,128)}, f32[1024,1024]{1,0:T(8,128)S(1)}) fusion(f32[1024,1024]{1,0:T(8,128)} %fusion.16, f32[1024,1024]{1,0:T(8,128)} %fusion.30, f32[1024,1024]{1,0:T(8,128)S(1)} %fusion.18, f32[]{:T(128)S(6)} %convert_element_type.54, bf16[2,2048,1024]{2,1,0:T(8,128)(2,1)} %constant.198.clone, s32[]{:T(128)S(6)} %select_n.164, ...), kind=kOutput, calls=%fused_computation.98 | convolution fusion | flops 4308598784 | bytes 29360136 | tf_op jit(solution)/shard_map/dot_general | solution.py:159
  130.7 2.6 copy.77
  135.9 4.2 fusion.283
  140.1 2.5 copy.72
  142.6 2.5 copy.73
  147.8 4.9 fusion.85
  155.3 2.0 fusion.80
  157.4 2.0 add_bitcast_fusion.10
  162.4 12.3 %reverse.25 = f32[1,512]{1,0:T(1,128)S(1)} reverse(f32[1,512]{1,0:T(1,128)S(1)} %bitcast.383), dimensions={1} | reverse | bytes 4096
  174.8 4.6 fusion.70
  183.6 2.1 add_bitcast_fusion.9
  190.6 2.6 broadcast_select_fusion.3
  193.2 6.4 %fusion.14 = f32[1024,1024]{1,0:T(8,128)S(1)} fusion(bf16[2,2048,1024]{2,1,0:T(8,128)(2,1)} %constant.199.clone, s32[]{:T(128)S(6)} %select_n.164, bf16[512,2048]{1,0:T(8,128)(2,1)S(1)} %get-tuple-element.64, bf16[512,2048]{1,0:T(8,128)(2,1)S(1)} %get-tuple-element.63), kind=kOutput, calls=%fused_computation.23 | convolution fusion | flops 4303355904 | bytes 12582916 | tf_op jit(solution)/shard_map/dot_general | solution.py:159
  199.7 6.1 %fusion.26 = f32[1024,1024]{1,0:T(8,128)} fusion(bf16[2,2048,1024]{2,1,0:T(8,128)(2,1)S(1)} %bitcast.412, s32[]{:T(128)S(6)} %select_n.164, bf16[512,2048]{1,0:T(8,128)(2,1)S(1)} %get-tuple-element.64, bf16[512,2048]{1,0:T(8,128)(2,1)S(1)} %get-tuple-element.63), kind=kOutput, calls=%fused_computation.35 | convolution fusion | flops 4303355904 | bytes 12582916 | tf_op jit(solution)/shard_map/dot_general | solution.py:159
  207.7 9.4 %fusion.12 = f32[1024,1024]{1,0:T(8,128)} fusion(bf16[2,2048,1024]{2,1,0:T(8,128)(2,1)} %constant.199.clone, s32[]{:T(128)S(6)} %select_n.164, bf16[512,2048]{1,0:T(8,128)(2,1)S(1)} %get-tuple-element.68, bf16[512,2048]{1,0:T(8,128)(2,1)S(1)} %get-tuple-element.67), kind=kOutput, calls=%fused_computation.21 | convolution fusion | flops 4303355904 | bytes 12582916 | tf_op jit(solution)/shard_map/dot_general | solution.py:159
  217.1 11.5 %add_add_fusion = (f32[1024,1024]{1,0:T(8,128)}, f32[1024,1024]{1,0:T(8,128)S(1)}) fusion(f32[1024,1024]{1,0:T(8,128)} %fusion.12, f32[1024,1024]{1,0:T(8,128)} %fusion.26, f32[1024,1024]{1,0:T(8,128)S(1)} %fusion.14, f32[]{:T(128)S(6)} %convert_element_type.54, bf16[2,2048,1024]{2,1,0:T(8,128)(2,1)} %constant.198.clone, s32[]{:T(128)S(6)} %select_n.164, ...), kind=kOutput, calls=%fused_computation.97 | convolution fusion | flops 4308598784 | bytes 29360136 | tf_op jit(solution)/shard_map/dot_general | solution.py:159
  228.6 2.1 fusion.286
  232.3 2.9 copy.85
  235.2 2.6 copy.86
  237.8 2.5 copy.87
  240.3 5.9 %fusion.51 = f32[512,1024]{1,0:T(8,128)} fusion(f32[1024,512]{1,0:T(8,128)} %constant.219, f32[512]{0:T(512)S(1)} %copy-done.57, f32[512]{0:T(512)S(1)} %copy-done.54, f32[1,512,512]{1,2,0:T(8,128)} %copy.86, f32[1,512,512]{1,2,0:T(8,128)} %copy.87, f32[1,512,512]{1,2,0:T(8,128)S(1)} %copy.84, f32[1,512,512]{1,2,0:T(8,128)} %copy.85), kind=kOutput, calls=%fused_computation.104 | convolution fusion | flops 1611923456 | bytes 8392704 | tf_op jit(solution)/shard_map/dot_general | solution.py:75
  246.3 3.3 fusion.61
  249.5 2.1 fusion.285
  253.2 2.6 copy.81
  255.8 2.5 copy.82
  258.3 2.5 copy.83
  260.9 4.6 fusion.66
  268.3 2.2 add_bitcast_fusion.6
  271.8 3.3 fusion.56
  281.8 4.5 add_bitcast_fusion.5
  293.7 5.0 %fusion.94 = f32[512,1024]{1,0:T(8,128)S(1)} fusion(f32[1024,512]{1,0:T(8,128)} %constant.227, f32[512]{0:T(512)S(1)} %bitcast.402, f32[512]{0:T(512)S(1)} %copy-done.63, f32[512]{0:T(512)S(1)} %copy-done.64, pred[512]{0:T(512)(128)(4,1)S(1)} %copy-done.68, f32[512]{0:T(512)S(1)} %bitcast.406, f32[512]{0:T(512)S(1)} %bitcast.403, ...), kind=kOutput, calls=%fused_computation.166 | convolution fusion | flops 1615069184 | bytes 6302208 | tf_op jit(solution)/shard_map/dot_general | solution.py:75
  298.7 2.8 add_bitcast_fusion
  301.5 2.7 fusion.105
  304.2 2.7 add_bitcast_fusion.1
  313.2 2.7 fusion.116
  315.9 2.8 add_bitcast_fusion.2
  318.7 2.7 fusion.127
  321.4 2.8 add_bitcast_fusion.3
  325.2 3.2 fusion.36
  328.5 2.7 slice_abs_fusion.1
  337.5 2.9 copy.69
  344.0 2.9 copy.70
  346.9 4.6 round-nearest-even_convert_fusion.1
  353.5 24.2 %collective-permute-done.10 = f32[2,4,1024]{2,1,0:T(4,128)S(1)} collective-permute-done((f32[2,4,1024]{2,1,0:T(4,128)S(1)}, f32[2,4,1024]{2,1,0:T(4,128)S(1)}, u32[]{:S(2)}, u32[]{:S(2)}) %collective-permute-start.10) | collective-permute-done | bytes 32800 | tf_op jit(solution)/shard_map/ppermute | solution.py:22
  381.8 21.6 %collective-permute-done.13 = f32[2,4,1024]{2,1,0:T(4,128)S(1)} collective-permute-done((f32[2,4,1024]{2,1,0:T(4,128)S(1)}, f32[2,4,1024]{2,1,0:T(4,128)S(1)}, u32[]{:S(2)}, u32[]{:S(2)}) %collective-permute-start.13) | collective-permute-done | bytes 32800 | tf_op jit(solution)/shard_map/ppermute | solution.py:22
  405.5 4.5 slice_add_fusion.1
  413.2 6.4 %fusion.8 = f32[256,2048]{1,0:T(8,128)S(1)} fusion(f32[2,1024,2048]{2,1,0:T(8,128)} %constant.214.clone, s32[]{:T(128)S(6)} %select_n.188, f32[2,256,1024]{1,2,0:T(8,128)S(1)} %copy-done.45), kind=kOutput, calls=%fused_computation.9 | convolution fusion | flops 3221225472 | bytes 11535360 | tf_op jit(solution)/shard_map/dot_general | solution.py:265
  419.6 6.3 %fusion.6 = f32[256,2048]{1,0:T(8,128)S(1)} fusion(f32[2,1024,2048]{2,1,0:T(8,128)} %constant.214.clone, s32[]{:T(128)S(6)} %select_n.188, f32[2,256,1024]{1,2,0:T(8,128)S(1)} %get-tuple-element.28), kind=kOutput, calls=%fused_computation.7 | convolution fusion | flops 3221225472 | bytes 11535360 | tf_op jit(solution)/shard_map/dot_general | solution.py:265
  425.9 6.8 %bitcast_reduce_fusion.1 = (f32[4,2048]{1,0:T(4,128)S(1)}, f32[256,2048]{1,0:T(8,128)S(1)}) fusion(f32[256,2048]{1,0:T(8,128)S(1)} %fusion.8, f32[256,1024]{0,1:T(8,128)} %collective-permute-done.11, f32[2,1024,2048]{2,1,0:T(8,128)} %constant.214.clone, s32[]{:T(128)S(6)} %select_n.192), kind=kOutput, calls=%fused_computation.66 | convolution fusion | flops 3222790144 | bytes 13664260 | tf_op jit(solution)/shard_map/dot_general | solution.py:265
  433.2 4.4 bitcast_reduce_fusion
  439.6 3.3 collective-permute-start.18
  443.4 40.6 %collective-permute-done.16 = f32[4,2048]{1,0:T(4,128)S(1)} collective-permute-done((f32[4,2048]{1,0:T(4,128)S(1)}, f32[4,2048]{1,0:T(4,128)S(1)}, u32[]{:S(2)}, u32[]{:S(2)}) %collective-permute-start.16) | collective-permute-done | bytes 32800 | tf_op jit(solution)/shard_map/ppermute | solution.py:17
  485.0 4.0 maximum_bitcast_fusion
  (285 shorter events, 86.9 us)
Async XLA Ops:
  2.6 8.6 %copy-start.62 = (s32[1,3]{1,0:T(1,128)S(1)}, s32[1,3]{1,0:T(1,128)}, u32[]{:S(2)}) copy-start(s32[1,3]{1,0:T(1,128)} %param.35) | copy-start | bytes 40
  6.7 49.7 %collective-permute-start.1 = (bf16[512,2048]{1,0:T(8,128)(2,1)}, bf16[512,2048]{1,0:T(8,128)(2,1)}, u32[]{:S(2)}, u32[]{:S(2)}) collective-permute-start(bf16[512,2048]{1,0:T(8,128)(2,1)} %get-tuple-element.52), channel_id=1, source_target_pairs={{0,8},{4,12},{8,0},{12,4},{1,9},{5,13},{9,1},{13,5},{2,10},{6,14},... | collective-permute-start | bytes 6291464 | tf_op jit(solution)/shard_map/ppermute | solution.py:22
  9.6 46.8 %collective-permute-start = (bf16[512,2048]{1,0:T(8,128)(2,1)S(1)}, bf16[512,2048]{1,0:T(8,128)(2,1)}, u32[]{:S(2)}, u32[]{:S(2)}) collective-permute-start(bf16[512,2048]{1,0:T(8,128)(2,1)S(1)} %get-tuple-element.51), channel_id=1, source_target_pairs={{0,4},{4,0},{8,12},{12,8},{1,5},{5,1},{9,13},{13,9},{2,6},{6,2},{1... | collective-permute-start | bytes 6291464 | tf_op jit(solution)/shard_map/ppermute | solution.py:31
  9.6 6.6 %collective-permute-start.3 = (s32[1,1]{1,0:T(1,128)}, s32[1,1]{1,0:T(1,128)}, u32[]{:S(2)}, u32[]{:S(2)}) collective-permute-start(s32[1,1]{1,0:T(1,128)} %get-tuple-element.113), channel_id=1, source_target_pairs={{0,1},{1,2},{2,3},{3,0},{4,5},{5,6},{6,7},{7,4},{8,9},{9,10},{10,1... | collective-permute-start | bytes 20 | tf_op jit(solution)/shard_map/ppermute | solution.py:17
  17.6 40.9 %slice-start.8 = ((s8[8388608]{0:T(1024)(128)(4,1)}), s8[4194304]{0:T(1024)(128)(4,1)S(1)}, s32[]{:S(2)}) async-start(s8[8388608]{0:T(1024)(128)(4,1)} %bitcast.413), calls=%async_computation.8 | async-start | bytes 8388608
  20.3 38.1 %slice-start.9 = ((s8[8388608]{0:T(1024)(128)(4,1)}), s8[4194304]{0:T(1024)(128)(4,1)S(1)}, s32[]{:S(2)}) async-start(s8[8388608]{0:T(1024)(128)(4,1)} %bitcast.413), calls=%async_computation.9 | async-start | bytes 8388608
  20.3 48.9 %collective-permute-start.4 = (bf16[512,2048]{1,0:T(8,128)(2,1)S(1)}, bf16[512,2048]{1,0:T(8,128)(2,1)}, u32[]{:S(2)}, u32[]{:S(2)}) collective-permute-start(bf16[512,2048]{1,0:T(8,128)(2,1)S(1)} %get-tuple-element.65), channel_id=1, source_target_pairs={{0,3},{1,0},{2,1},{3,2},{4,7},{5,4},{6,5},{7,6},{8,11},{9,8},{10,9... | collective-permute-start | bytes 6291464 | tf_op jit(solution)/shard_map/ppermute | solution.py:17
  22.6 77.9 %collective-permute-start.6 = (bf16[512,2048]{1,0:T(8,128)(2,1)S(1)}, bf16[512,2048]{1,0:T(8,128)(2,1)}, u32[]{:S(2)}, u32[]{:S(2)}) collective-permute-start(bf16[512,2048]{1,0:T(8,128)(2,1)S(1)} %get-tuple-element.66), channel_id=1, source_target_pairs={{0,8},{4,12},{8,0},{12,4},{1,9},{5,13},{9,1},{13,5},{2,10},{6,14},... | collective-permute-start | bytes 6291464 | tf_op jit(solution)/shard_map/ppermute | solution.py:22
  56.4 48.1 %collective-permute-start.2 = (bf16[512,2048]{1,0:T(8,128)(2,1)}, bf16[512,2048]{1,0:T(8,128)(2,1)S(1)}, u32[]{:S(2)}, u32[]{:S(2)}) collective-permute-start(bf16[512,2048]{1,0:T(8,128)(2,1)} %collective-permute-done.1), channel_id=1, source_target_pairs={{0,4},{4,0},{8,12},{12,8},{1,5},{5,1},{9,13},{13,9},{2,6},{6,2},{1... | collective-permute-start | bytes 6291464 | tf_op jit(solution)/shard_map/ppermute | solution.py:31
  56.4 6.6 %slice-start.4 = ((s8[8388608]{0:T(1024)(128)(4,1)}), s8[4194304]{0:T(1024)(128)(4,1)S(1)}, s32[]{:S(2)}) async-start(s8[8388608]{0:T(1024)(128)(4,1)} %bitcast.409), calls=%async_computation.4 | async-start | bytes 8388608
  58.5 4.5 slice-start.5
  69.2 121.4 %collective-permute-start.5 = (bf16[512,2048]{1,0:T(8,128)(2,1)}, bf16[512,2048]{1,0:T(8,128)(2,1)}, u32[]{:S(2)}, u32[]{:S(2)}) collective-permute-start(bf16[512,2048]{1,0:T(8,128)(2,1)} %collective-permute-done.4), channel_id=1, source_target_pairs={{0,4},{4,0},{8,12},{12,8},{1,5},{5,1},{9,13},{13,9},{2,6},{6,2},{1... | collective-permute-start | bytes 6291464 | tf_op jit(solution)/shard_map/ppermute | solution.py:31
  100.5 90.0 %collective-permute-start.7 = (bf16[512,2048]{1,0:T(8,128)(2,1)}, bf16[512,2048]{1,0:T(8,128)(2,1)}, u32[]{:S(2)}, u32[]{:S(2)}) collective-permute-start(bf16[512,2048]{1,0:T(8,128)(2,1)} %collective-permute-done.6), channel_id=1, source_target_pairs={{0,3},{1,0},{2,1},{3,2},{4,7},{5,4},{6,5},{7,6},{8,11},{9,8},{10,9... | collective-permute-start | bytes 6291464 | tf_op jit(solution)/shard_map/ppermute | solution.py:17
  147.8 4.9 %copy-start = (f32[1024,512]{1,0:T(8,128)S(1)}, f32[1024,512]{1,0:T(8,128)}, u32[]{:S(2)}) copy-start(f32[1024,512]{1,0:T(8,128)} %constant.220) | copy-start | bytes 6291460
  147.8 4.9 %copy-start.23 = (f32[1,512,512]{1,2,0:T(8,128)S(1)}, f32[1,512,512]{1,2,0:T(8,128)}, u32[]{:S(2)}) copy-start(f32[1,512,512]{1,2,0:T(8,128)} %copy.72) | copy-start | bytes 3145732
  147.8 4.9 %copy-start.25 = (f32[1,512,512]{1,2,0:T(8,128)S(1)}, f32[1,512,512]{1,2,0:T(8,128)}, u32[]{:S(2)}) copy-start(f32[1,512,512]{1,2,0:T(8,128)} %copy.73) | copy-start | bytes 3145732
  147.8 4.9 %copy-start.27 = (f32[1,512,512]{1,2,0:T(8,128)S(1)}, f32[1,512,512]{1,2,0:T(8,128)}, u32[]{:S(2)}) copy-start(f32[1,512,512]{1,2,0:T(8,128)} %copy.74) | copy-start | bytes 3145732
  147.8 4.9 %copy-start.29 = (f32[1,512,512]{1,2,0:T(8,128)S(1)}, f32[1,512,512]{1,2,0:T(8,128)}, u32[]{:S(2)}) copy-start(f32[1,512,512]{1,2,0:T(8,128)} %copy.75) | copy-start | bytes 3145732
  155.3 4.1 copy-start.31
  157.3 17.4 %copy-start.54 = (f32[512]{0:T(512)S(1)}, f32[512]{0:T(512)}, u32[]{:S(2)}) copy-start(f32[512]{0:T(512)} %constant.225) | copy-start | bytes 6148
  157.3 17.4 %copy-start.57 = (f32[512]{0:T(512)S(1)}, f32[512]{0:T(512)}, u32[]{:S(2)}) copy-start(f32[512]{0:T(512)} %constant.226) | copy-start | bytes 6148
  174.8 4.7 copy-start.2
  174.8 4.7 copy-start.24
  174.8 4.7 copy-start.26
  174.8 4.7 copy-start.28
  174.8 4.7 copy-start.30
  174.8 4.7 copy-start.55
  174.8 4.7 copy-start.56
  190.5 15.3 %collective-permute-start.8 = (bf16[512,2048]{1,0:T(8,128)(2,1)}, bf16[512,2048]{1,0:T(8,128)(2,1)S(1)}, u32[]{:S(2)}, u32[]{:S(2)}) collective-permute-start(bf16[512,2048]{1,0:T(8,128)(2,1)} %collective-permute-done.7), channel_id=1, source_target_pairs={{0,4},{4,0},{8,12},{12,8},{1,5},{5,1},{9,13},{13,9},{2,6},{6,2},{1... | collective-permute-start | bytes 6291464 | tf_op jit(solution)/shard_map/ppermute | solution.py:31
  190.6 9.1 %slice-start.6 = ((s8[8388608]{0:T(1024)(128)(4,1)}), s8[4194304]{0:T(1024)(128)(4,1)S(1)}, s32[]{:S(2)}) async-start(s8[8388608]{0:T(1024)(128)(4,1)} %bitcast.411), calls=%async_computation.6 | async-start | bytes 8388608
  193.2 6.5 %slice-start.7 = ((s8[8388608]{0:T(1024)(128)(4,1)}), s8[4194304]{0:T(1024)(128)(4,1)S(1)}, s32[]{:S(2)}) async-start(s8[8388608]{0:T(1024)(128)(4,1)} %bitcast.411), calls=%async_computation.7 | async-start | bytes 8388608
  232.3 13.9 %copy-start.7 = (f32[1,512,512]{1,2,0:T(8,128)}, f32[1,512,512]{1,2,0:T(8,128)S(1)}, u32[]{:S(2)}) copy-start(f32[1,512,512]{1,2,0:T(8,128)S(1)} %copy.84) | copy-start | bytes 3145732
  240.3 5.9 %copy-start.3 = (f32[1024,512]{1,0:T(8,128)S(1)}, f32[1024,512]{1,0:T(8,128)}, u32[]{:S(2)}) copy-start(f32[1024,512]{1,0:T(8,128)} %constant.219) | copy-start | bytes 6291460
  240.3 5.9 %copy-start.12 = (f32[1,512,512]{1,2,0:T(8,128)S(1)}, f32[1,512,512]{1,2,0:T(8,128)}, u32[]{:S(2)}) copy-start(f32[1,512,512]{1,2,0:T(8,128)} %copy.85) | copy-start | bytes 3145732
  240.3 5.9 %copy-start.16 = (f32[1,512,512]{1,2,0:T(8,128)S(1)}, f32[1,512,512]{1,2,0:T(8,128)}, u32[]{:S(2)}) copy-start(f32[1,512,512]{1,2,0:T(8,128)} %copy.86) | copy-start | bytes 3145732
  240.3 5.9 %copy-start.21 = (f32[1,512,512]{1,2,0:T(8,128)S(1)}, f32[1,512,512]{1,2,0:T(8,128)}, u32[]{:S(2)}) copy-start(f32[1,512,512]{1,2,0:T(8,128)} %copy.87) | copy-start | bytes 3145732
  246.2 3.3 copy-start.48
  260.9 4.6 copy-start.6
  260.9 4.6 copy-start.9
  260.9 4.6 copy-start.18
  268.3 3.4 copy-start.4
  271.8 3.3 copy-start.38
  281.8 10.3 %copy-start.59 = (s32[512]{0:T(512)S(1)}, s32[512]{0:T(512)}, u32[]{:S(2)}) copy-start(s32[512]{0:T(512)} %iota_multiply_fusion) | copy-start | bytes 6148
  281.8 11.8 %copy-start.63 = (f32[512]{0:T(512)S(1)}, f32[512]{0:T(512)}, u32[]{:S(2)}) copy-start(f32[512]{0:T(512)} %get-tuple-element.121) | copy-start | bytes 6148
  281.8 11.8 %copy-start.64 = (f32[512]{0:T(512)S(1)}, f32[512]{0:T(512)}, u32[]{:S(2)}) copy-start(f32[512]{0:T(512)} %get-tuple-element.122) | copy-start | bytes 6148
  281.8 11.8 %copy-start.68 = (pred[512]{0:T(512)(128)(4,1)S(1)}, pred[512]{0:T(512)(128)(4,1)}, u32[]{:S(2)}) copy-start(pred[512]{0:T(512)(128)(4,1)} %fusion.252) | copy-start | bytes 1540
  293.6 5.0 %copy-start.51 = (f32[512,512]{0,1:T(8,128)S(1)}, f32[512,512]{0,1:T(8,128)}, u32[]{:S(2)}) copy-start(f32[512,512]{0,1:T(8,128)} %get-tuple-element.33) | copy-start | bytes 3145732
  293.6 5.0 %copy-start.52 = (f32[512,512]{0,1:T(8,128)S(1)}, f32[512,512]{0,1:T(8,128)}, u32[]{:S(2)}) copy-start(f32[512,512]{0,1:T(8,128)} %get-tuple-element.34) | copy-start | bytes 3145732
  293.6 5.0 %copy-start.66 = (f32[1024,512]{1,0:T(8,128)S(1)}, f32[1024,512]{1,0:T(8,128)}, u32[]{:S(2)}) copy-start(f32[1024,512]{1,0:T(8,128)} %constant.228) | copy-start | bytes 6291460
  328.4 3.3 copy-start.5
  351.5 26.2 %collective-permute-start.9 = (s16[2,256,1024]{1,2,0:T(8,128)(2,1)S(1)}, s16[2,256,1024]{1,2,0:T(8,128)(2,1)S(1)}, u32[]{:S(2)}, u32[]{:S(2)}) collective-permute-start(s16[2,256,1024]{1,2,0:T(8,128)(2,1)S(1)} %get-tuple-element.29), channel_id=1, source_target_pairs={{0,8},{4,12},{8,0},{12,4},{1,9},{5,13},{9,1},{13,5},{2,10},{6,14},... | collective-permute-start | bytes 3145736 | tf_op jit(solution)/shard_map/ppermute | solution.py:22
  353.0 24.7 %collective-permute-start.10 = (f32[2,4,1024]{2,1,0:T(4,128)S(1)}, f32[2,4,1024]{2,1,0:T(4,128)S(1)}, u32[]{:S(2)}, u32[]{:S(2)}) collective-permute-start(f32[2,4,1024]{2,1,0:T(4,128)S(1)} %get-tuple-element.89), channel_id=1, source_target_pairs={{0,8},{4,12},{8,0},{12,4},{1,9},{5,13},{9,1},{13,5},{2,10},{6,14},... | collective-permute-start | bytes 98312 | tf_op jit(solution)/shard_map/ppermute | solution.py:22
  377.7 27.8 %collective-permute-start.12 = (s16[2,256,1024]{1,2,0:T(8,128)(2,1)}, s16[2,256,1024]{1,2,0:T(8,128)(2,1)}, u32[]{:S(2)}, u32[]{:S(2)}) collective-permute-start(s16[2,256,1024]{1,2,0:T(8,128)(2,1)} %get-tuple-element.7), channel_id=1, source_target_pairs={{0,8},{4,12},{8,0},{12,4},{1,9},{5,13},{9,1},{13,5},{2,10},{6,14},... | collective-permute-start | bytes 3145736 | tf_op jit(solution)/shard_map/ppermute | solution.py:22
  379.3 24.2 %collective-permute-start.13 = (f32[2,4,1024]{2,1,0:T(4,128)S(1)}, f32[2,4,1024]{2,1,0:T(4,128)S(1)}, u32[]{:S(2)}, u32[]{:S(2)}) collective-permute-start(f32[2,4,1024]{2,1,0:T(4,128)S(1)} %get-tuple-element.8), channel_id=1, source_target_pairs={{0,8},{4,12},{8,0},{12,4},{1,9},{5,13},{9,1},{13,5},{2,10},{6,14},... | collective-permute-start | bytes 98312 | tf_op jit(solution)/shard_map/ppermute | solution.py:22
  411.4 14.4 %collective-permute-start.11 = (f32[256,1024]{0,1:T(8,128)S(1)}, f32[256,1024]{0,1:T(8,128)}, u32[]{:S(2)}, u32[]{:S(2)}) collective-permute-start(f32[256,1024]{0,1:T(8,128)S(1)} %dynamic-slice_bitcast_fusion.5), channel_id=1, source_target_pairs={{0,4},{4,0},{8,12},{12,8},{1,5},{5,1},{9,13},{13,9},{2,6},{6,2},{1... | collective-permute-start | bytes 3145736 | tf_op jit(solution)/shard_map/ppermute | solution.py:31
  411.7 21.5 %collective-permute-start.14 = (f32[256,1024]{0,1:T(8,128)S(1)}, f32[256,1024]{0,1:T(8,128)S(1)}, u32[]{:S(2)}, u32[]{:S(2)}) collective-permute-start(f32[256,1024]{0,1:T(8,128)S(1)} %dynamic-slice_bitcast_fusion.4), channel_id=1, source_target_pairs={{0,4},{4,0},{8,12},{12,8},{1,5},{5,1},{9,13},{13,9},{2,6},{6,2},{1... | collective-permute-start | bytes 3145736 | tf_op jit(solution)/shard_map/ppermute | solution.py:31
  413.2 20.0 %slice-start = ((s8[16777216]{0:T(1024)(128)(4,1)}), s8[4194304]{0:T(1024)(128)(4,1)S(1)}, s32[]{:S(2)}) async-start(s8[16777216]{0:T(1024)(128)(4,1)} %bitcast.363), calls=%async_computation | async-start | bytes 8388608
  413.2 20.0 %slice-start.1 = ((s8[16777216]{0:T(1024)(128)(4,1)}), s8[4194304]{0:T(1024)(128)(4,1)S(1)}, s32[]{:S(2)}) async-start(s8[16777216]{0:T(1024)(128)(4,1)} %bitcast.363), calls=%async_computation.1 | async-start | bytes 8388608
  419.6 13.6 %slice-start.2 = ((s8[16777216]{0:T(1024)(128)(4,1)}), s8[4194304]{0:T(1024)(128)(4,1)S(1)}, s32[]{:S(2)}) async-start(s8[16777216]{0:T(1024)(128)(4,1)} %bitcast.363), calls=%async_computation.2 | async-start | bytes 8388608
  425.9 7.3 %slice-start.3 = ((s8[16777216]{0:T(1024)(128)(4,1)}), s8[4194304]{0:T(1024)(128)(4,1)S(1)}, s32[]{:S(2)}) async-start(s8[16777216]{0:T(1024)(128)(4,1)} %bitcast.363), calls=%async_computation.3 | async-start | bytes 8388608
  433.1 50.9 %collective-permute-start.15 = (s16[256,2048]{1,0:T(8,128)(2,1)S(1)}, s16[256,2048]{1,0:T(8,128)(2,1)S(1)}, u32[]{:S(2)}, u32[]{:S(2)}) collective-permute-start(s16[256,2048]{1,0:T(8,128)(2,1)S(1)} %fusion.47), channel_id=1, source_target_pairs={{0,1},{1,2},{2,3},{3,0},{4,5},{5,6},{6,7},{7,4},{8,9},{9,10},{10,1... | collective-permute-start | bytes 3145736 | tf_op jit(solution)/shard_map/ppermute | solution.py:17
  437.9 46.4 %collective-permute-start.17 = (s16[256,2048]{1,0:T(8,128)(2,1)S(1)}, s16[256,2048]{1,0:T(8,128)(2,1)S(1)}, u32[]{:S(2)}, u32[]{:S(2)}) collective-permute-start(s16[256,2048]{1,0:T(8,128)(2,1)S(1)} %fusion.45), channel_id=1, source_target_pairs={{0,1},{1,2},{2,3},{3,0},{4,5},{5,6},{6,7},{7,4},{8,9},{9,10},{10,1... | collective-permute-start | bytes 3145736 | tf_op jit(solution)/shard_map/ppermute | solution.py:17
  438.0 46.0 %collective-permute-start.16 = (f32[4,2048]{1,0:T(4,128)S(1)}, f32[4,2048]{1,0:T(4,128)S(1)}, u32[]{:S(2)}, u32[]{:S(2)}) collective-permute-start(f32[4,2048]{1,0:T(4,128)S(1)} %get-tuple-element.85), channel_id=1, source_target_pairs={{0,1},{1,2},{2,3},{3,0},{4,5},{5,6},{6,7},{7,4},{8,9},{9,10},{10,1... | collective-permute-start | bytes 98312 | tf_op jit(solution)/shard_map/ppermute | solution.py:17
  439.6 44.8 %collective-permute-start.18 = (f32[4,2048]{1,0:T(4,128)S(1)}, f32[4,2048]{1,0:T(4,128)S(1)}, u32[]{:S(2)}, u32[]{:S(2)}) collective-permute-start(f32[4,2048]{1,0:T(4,128)S(1)} %get-tuple-element.87), channel_id=1, source_target_pairs={{0,1},{1,2},{2,3},{3,0},{4,5},{5,6},{6,7},{7,4},{8,9},{9,10},{10,1... | collective-permute-start | bytes 98312 | tf_op jit(solution)/shard_map/ppermute | solution.py:17
  (34 other events, 72.3 us)

commit v3 on v2

--- a/solution.py
+++ b/solution.py
@@ -92,8 +92,10 @@
 
 
 def mirrored(vec):
-    flipped = vec[:, ::-1]
-    return jnp.stack([jnp.roll(flipped[0], 1), flipped[3], flipped[2], flipped[1]])
+    turn = np.eye(vec.shape[1], dtype=np.float32)[::-1]
+    flipped = jnp.dot(vec, turn, precision=lax.Precision.HIGHEST)
+    rolled = jnp.dot(vec, np.roll(turn, 1, axis=1), precision=lax.Precision.HIGHEST)
+    return jnp.stack([rolled[0], flipped[3], flipped[2], flipped[1]])
 
 
 def cross(nr, ni, fr, fi, scale):
@@ -159,16 +161,21 @@
         spec = jnp.dot(pixels, table_hi, preferred_element_type=jnp.float32) + jnp.dot(
             pixels, table_lo, preferred_element_type=jnp.float32
         )
-        return spec.reshape(2, quarter, 2 * columns)
+        return spec
 
     twist_cos, twist_sin = twist_table(height)
     forward_table = column_table(quarter, -1.0)
 
     def column_pass(own, other):
-        even = own + other
-        odd = (own - other) * sign
-        er, ei = even[..., :columns], even[..., columns:]
-        dr, di = odd[..., :columns], odd[..., columns:]
+        def cut(j, part):
+            where = (slice(j * quarter, (j + 1) * quarter), slice(part * columns, (part + 1) * columns))
+            a, b = own[where], other[where]
+            return a + b, (a - b) * sign
+
+        er, ei, dr, di = [None] * 2, [None] * 2, [None] * 2, [None] * 2
+        for j in range(2):
+            er[j], dr[j] = cut(j, 0)
+            ei[j], di[j] = cut(j, 1)
         parts = [
             (er[0] + er[1], ei[0] + ei[1]),
             (dr[0] + di[1], di[0] - dr[1]),
@@ -252,6 +259,9 @@
         if c > 0:
             sent, got = lax.optimization_barrier((sent, got))
         got = tuple(swap_groups(v, members) for v in sent)
+        tables = inverse_table
+        if c > 0:
+            tables, got, result = lax.optimization_barrier((tables, got, result))
         total = own[:, cut] + decode(*got)
         result = None
         for s in range(members):
@@ -260,7 +270,7 @@
             if s > 0:
                 block = shift_members(block, members, s)
             table = lax.dynamic_index_in_dim(
-                inverse_table, (member - s) % members, 0, keepdims=False
+                tables, (member - s) % members, 0, keepdims=False
             )
             term = jnp.dot(block, table, precision=HIGH)
             result = term if result is None else result + term

time: 490 us -> 391 us (0.80); the launches traced: 489 us -> 385 us
  local copies, waits for them, and re-layouts: 103 us -> 11 us
  waiting for transfers between devices: 151 us -> 139 us
  matrix products: 162 us -> 172 us
  other arithmetic: 46 us -> 36.9 us
    unnamed x182 -> x64, local copies, waits for them, and re-layouts: 58.8 us -> 1.2 us
    slice x24 -> x4, local copies, waits for them, and re-layouts: 17 us -> 0.04 us  [mirrored(): return jnp.stack([rolled[0], flipped[3], flipped[2], flipped[1]])]
    dot_general x24, matrix products: 73.3 us -> 85.6 us  [split(): return jnp.dot(a, b, precision=HIGH)]
    mul x8 -> x0, local copies, waits for them, and re-layouts: 12.2 us -> none  [the longest x4 8.07 us: encode(): coded = jnp.round(grouped * (32767.0 / peak)).astype(jnp.int16)]
    ppermute x6, waiting for transfers between devices: 110 us -> 100 us  [swap_groups(): lax.ppermute(value, 'pencil', [(s, (s + members) % count) for s in range(...]
    dot_general x4, matrix products: 35.4 us -> 27.3 us  [row_pass(): jnp.dot(pixels, table_hi, preferred_element_type=jnp.float32)]
    add x0 -> x2, other arithmetic: none -> 6.02 us  [cut(): return (a + b, (a - b) * sign)]
  transfers between devices with their start and end apart: 19 -> 19, of which waited for: 5 -> 7; matrix products, arithmetic and copies ran while one was open for 30% -> 24% of each run, Pallas kernels for 0% -> 0%
where the time goes in v3:
time: 391 us; the launch traced here: 385 us
  matrix products  172 us (44%)
  waiting for transfers between devices  139 us (36%)
  other arithmetic  36.9 us (9%)
  starting transfers between devices  19.1 us (5%)
  local copies, waits for them, and re-layouts  11 us (3%)
  between operations  6 us (2%)
    ppermute x6, waiting for transfers between devices, swap_groups(): lax.ppermute(value, 'pencil', [(s, (s + members) % count) for s in range(...  100 us
    dot_general x24, matrix products, split(): return jnp.dot(a, b, precision=HIGH)  85.6 us
    ppermute x7, waiting for transfers between devices, shift_tile(): lax.ppermute(value, 'tile', [(s, (s + steps) % count) for s in range(coun...  35.8 us
    dot_general x4, matrix products, row_pass(): jnp.dot(pixels, table_lo, preferred_element_type=jnp.float32)  31.9 us
    dot_general x4, matrix products, row_pass(): jnp.dot(pixels, table_hi, preferred_element_type=jnp.float32)  27.3 us
    dot_general x4, matrix products, shards(): term = jnp.dot(block, table, precision=HIGH)  22.5 us
    ppermute x7, starting transfers between devices, shift_tile(): lax.ppermute(value, 'tile', [(s, (s + steps) % count) for s in range(coun...  10.8 us
  transfers between devices with their start and end apart: 19, of which 7 were waited for; matrix products, arithmetic and copies ran while one was open for 24% of the time, Pallas kernels for 0%

profile of v3, /device:TPU:0, one launch (start us, length us, event | category | flops | bytes accessed | tf_op | source)
XLA Modules:
  0.0 384.5 jit_solution(3595580733809173640)
XLA Ops:
  0.0 1.3 fusion.329
  2.6 4.0 %dynamic-slice_bitcast_fusion.3 = (bf16[512,2048]{1,0:T(8,128)(2,1)S(1)}, bf16[512,2048]{1,0:T(8,128)(2,1)}) fusion(bf16[1,2,512,2048]{3,2,1,0:T(8,128)(2,1)} %param.41, s32[]{:T(128)S(6)} %select_n.161, s32[]{:T(128)S(6)} %select_n.165), kind=kLoop, calls=%fused_computation.90 | loop fusion | bytes 8388616 | tf_op jit(solution)/shard_map/jit(dynamic_index_in_dim)/squeeze | solution.py:131
  6.6 3.0 collective-permute-start.1
  9.6 1.6 collective-permute-start.3
  14.9 1.2 fusion.287
  17.4 2.5 dynamic-slice_bitcast_fusion.1
  20.5 2.0 collective-permute-start.4
  22.5 33.9 %collective-permute-done.1 = bf16[512,2048]{1,0:T(8,128)(2,1)} collective-permute-done((bf16[512,2048]{1,0:T(8,128)(2,1)}, bf16[512,2048]{1,0:T(8,128)(2,1)}, u32[]{:S(2)}, u32[]{:S(2)}) %collective-permute-start.1) | collective-permute-done | bytes 2097184 | tf_op jit(solution)/shard_map/ppermute | solution.py:22
  56.4 2.0 broadcast_select_fusion.7
  58.4 6.5 %fusion.18 = f32[1024,1024]{1,0:T(8,128)S(1)} fusion(bf16[2,2048,1024]{2,1,0:T(8,128)(2,1)} %constant.203.clone, s32[]{:T(128)S(6)} %select_n.164, bf16[512,2048]{1,0:T(8,128)(2,1)S(1)} %get-tuple-element.58, bf16[512,2048]{1,0:T(8,128)(2,1)S(1)} %get-tuple-element.57), kind=kOutput, calls=%fused_computation.27 | convolution fusion | flops 4303355904 | bytes 12582916 | tf_op jit(solution)/shard_map/dot_general | solution.py:161
  64.9 4.5 %fusion.52 = f32[1024,1024]{1,0:T(8,128)S(1)} fusion(f32[1024,1024]{1,0:T(8,128)S(1)} %fusion.18, bf16[2,2048,1024]{2,1,0:T(8,128)(2,1)S(1)} %bitcast.266, s32[]{:T(128)S(6)} %select_n.164, bf16[512,2048]{1,0:T(8,128)(2,1)S(1)} %get-tuple-element.58, bf16[512,2048]{1,0:T(8,128)(2,1)S(1)} %get-tuple-element.57), kind=kOutput, calls=%fused_computation.101 | convolution fusion | flops 4304404480 | bytes 16777220 | tf_op jit(solution)/shard_map/dot_general | solution.py:161
  69.4 31.1 %collective-permute-done.6 = bf16[512,2048]{1,0:T(8,128)(2,1)} collective-permute-done((bf16[512,2048]{1,0:T(8,128)(2,1)S(1)}, bf16[512,2048]{1,0:T(8,128)(2,1)}, u32[]{:S(2)}, u32[]{:S(2)}) %collective-permute-start.6) | collective-permute-done | bytes 2097184 | tf_op jit(solution)/shard_map/ppermute | solution.py:22
  100.5 3.8 collective-permute-start.7
  104.3 2.1 broadcast_select_fusion.5
  106.5 6.5 %fusion.16 = f32[1024,1024]{1,0:T(8,128)S(1)} fusion(bf16[2,2048,1024]{2,1,0:T(8,128)(2,1)} %constant.203.clone, s32[]{:T(128)S(6)} %select_n.164, bf16[512,2048]{1,0:T(8,128)(2,1)S(1)} %get-tuple-element.62, bf16[512,2048]{1,0:T(8,128)(2,1)S(1)} %get-tuple-element.61), kind=kOutput, calls=%fused_computation.25 | convolution fusion | flops 4303355904 | bytes 12582916 | tf_op jit(solution)/shard_map/dot_general | solution.py:161
  113.0 4.6 %fusion.55 = f32[1024,1024]{1,0:T(8,128)S(1)} fusion(f32[1024,1024]{1,0:T(8,128)S(1)} %fusion.16, bf16[2,2048,1024]{2,1,0:T(8,128)(2,1)S(1)} %bitcast.266, s32[]{:T(128)S(6)} %select_n.164, bf16[512,2048]{1,0:T(8,128)(2,1)S(1)} %get-tuple-element.62, bf16[512,2048]{1,0:T(8,128)(2,1)S(1)} %get-tuple-element.61), kind=kOutput, calls=%fused_computation.102 | convolution fusion | flops 4304404480 | bytes 16777220 | tf_op jit(solution)/shard_map/dot_general | solution.py:161
  117.6 1.5 slice_add_fusion.8
  119.2 3.9 %fusion.141 = f32[512,1024]{1,0:T(8,128)S(1)} fusion(f32[1024,512]{1,0:T(8,128)S(1)} %copy-done.1, f32[512]{0:T(512)S(1)} %copy-done.13, f32[512]{0:T(512)S(1)} %copy-done.8, f32[512,512]{1,0:T(8,128)S(1)} %get-tuple-element.27, f32[512,512]{1,0:T(8,128)S(1)} %get-tuple-element.26, f32[512,512]{1,0:T(8,128)S(1)} %get-tuple-element.25, ...), kind=kOutput, calls=%fused_computation.216 | convolution fusion | flops 1611923456 | bytes 8392704 | tf_op jit(solution)/shard_map/dot_general | solution.py:75
  123.1 3.9 %add_bitcast_fusion.8 = f32[1024,512]{0,1:T(8,128)S(1)} fusion(f32[512,1024]{1,0:T(8,128)S(1)} %fusion.141, f32[1024,512]{1,0:T(8,128)S(1)} %copy-done, f32[512]{0:T(512)S(1)} %copy-done.13, f32[512]{0:T(512)S(1)} %copy-done.8, f32[512,512]{1,0:T(8,128)S(1)} %get-tuple-element.27, f32[512,512]{1,0:T(8,128)S(1)} %get-tuple-element.26, ...), kind=kOutput, calls=%fused_computation.83 | convolution fusion | flops 1612447744 | bytes 10489856 | tf_op jit(solution)/shard_map/dot_general | solution.py:75
  127.1 4.0 %fusion.161 = f32[512,1024]{1,0:T(8,128)S(1)} fusion(f32[1024,512]{1,0:T(8,128)S(1)} %copy-done.1, f32[512,512]{1,0:T(8,128)S(1)} %get-tuple-element.30, f32[512,512]{1,0:T(8,128)S(1)} %get-tuple-element.29, f32[512,512]{1,0:T(8,128)S(1)} %get-tuple-element.31, f32[512,512]{1,0:T(8,128)S(1)} %get-tuple-element.24), kind=kOutput, calls=%fused_computation.240 | convolution fusion | flops 1611661312 | bytes 8388608 | tf_op jit(solution)/shard_map/dot_general | solution.py:75
  131.2 4.0 %fusion.148 = f32[512,1024]{1,0:T(8,128)S(1)} fusion(f32[1024,512]{1,0:T(8,128)S(1)} %copy-done.1, f32[512]{0:T(512)S(1)} %copy-done.12, f32[512]{0:T(512)S(1)} %copy-done.10, f32[512,512]{1,0:T(8,128)S(1)} %get-tuple-element.30, f32[512,512]{1,0:T(8,128)S(1)} %get-tuple-element.29, f32[512,512]{1,0:T(8,128)S(1)} %get-tuple-element.31, ...), kind=kOutput, calls=%fused_computation.223 | convolution fusion | flops 1611923456 | bytes 8392704 | tf_op jit(solution)/shard_map/dot_general | solution.py:75
  135.2 3.9 %fusion.155 = f32[512,1024]{1,0:T(8,128)S(1)} fusion(f32[1024,512]{1,0:T(8,128)S(1)} %copy-done.1, f32[512]{0:T(512)S(1)} %copy-done.11, f32[512]{0:T(512)S(1)} %copy-done.9, f32[512,512]{1,0:T(8,128)S(1)} %get-tuple-element.27, f32[512,512]{1,0:T(8,128)S(1)} %get-tuple-element.26, f32[512,512]{1,0:T(8,128)S(1)} %get-tuple-element.25, ...), kind=kOutput, calls=%fused_computation.230 | convolution fusion | flops 1611923456 | bytes 8392704 | tf_op jit(solution)/shard_map/dot_general | solution.py:75
  139.1 3.8 add_bitcast_fusion.11
  142.9 4.0 %add_bitcast_fusion.9 = f32[1024,512]{0,1:T(8,128)S(1)} fusion(f32[512,1024]{1,0:T(8,128)S(1)} %fusion.148, f32[1024,512]{1,0:T(8,128)S(1)} %copy-done, f32[512]{0:T(512)S(1)} %copy-done.12, f32[512]{0:T(512)S(1)} %copy-done.10, f32[512,512]{1,0:T(8,128)S(1)} %get-tuple-element.30, f32[512,512]{1,0:T(8,128)S(1)} %get-tuple-element.29, ...), kind=kOutput, calls=%fused_computation.84 | convolution fusion | flops 1612447744 | bytes 10489856 | tf_op jit(solution)/shard_map/dot_general | solution.py:75
  147.0 3.9 %add_bitcast_fusion.10 = f32[1024,512]{0,1:T(8,128)S(1)} fusion(f32[512,1024]{1,0:T(8,128)S(1)} %fusion.155, f32[1024,512]{1,0:T(8,128)S(1)} %copy-done, f32[512]{0:T(512)S(1)} %copy-done.11, f32[512]{0:T(512)S(1)} %copy-done.9, f32[512,512]{1,0:T(8,128)S(1)} %get-tuple-element.27, f32[512,512]{1,0:T(8,128)S(1)} %get-tuple-element.26, ...), kind=kOutput, calls=%fused_computation.85 | convolution fusion | flops 1612447744 | bytes 10489856 | tf_op jit(solution)/shard_map/dot_general | solution.py:75
  154.0 1.5 collective-permute-done.8
  155.5 3.3 broadcast_select_fusion.1
  158.8 9.4 %fusion.12 = f32[1024,1024]{1,0:T(8,128)} fusion(bf16[2,2048,1024]{2,1,0:T(8,128)(2,1)} %constant.203.clone, s32[]{:T(128)S(6)} %select_n.164, bf16[512,2048]{1,0:T(8,128)(2,1)S(1)} %get-tuple-element.68, bf16[512,2048]{1,0:T(8,128)(2,1)S(1)} %get-tuple-element.67), kind=kOutput, calls=%fused_computation.21 | convolution fusion | flops 4303355904 | bytes 12582916 | tf_op jit(solution)/shard_map/dot_general | solution.py:161
  168.2 10.2 %fusion.61 = f32[1024,1024]{1,0:T(8,128)} fusion(f32[1024,1024]{1,0:T(8,128)} %fusion.12, bf16[2,2048,1024]{2,1,0:T(8,128)(2,1)} %constant.202.clone, s32[]{:T(128)S(6)} %select_n.164, bf16[512,2048]{1,0:T(8,128)(2,1)S(1)} %get-tuple-element.68, bf16[512,2048]{1,0:T(8,128)(2,1)S(1)} %get-tuple-element.67), kind=kOutput, calls=%fused_computation.104 | convolution fusion | flops 4304404480 | bytes 16777220 | tf_op jit(solution)/shard_map/dot_general | solution.py:161
  178.5 9.5 %fusion.14 = f32[1024,1024]{1,0:T(8,128)} fusion(bf16[2,2048,1024]{2,1,0:T(8,128)(2,1)} %constant.203.clone, s32[]{:T(128)S(6)} %select_n.164, bf16[512,2048]{1,0:T(8,128)(2,1)S(1)} %get-tuple-element.135, bf16[512,2048]{1,0:T(8,128)(2,1)S(1)} %get-tuple-element.136), kind=kOutput, calls=%fused_computation.23 | convolution fusion | flops 4303355904 | bytes 12582916 | tf_op jit(solution)/shard_map/dot_general | solution.py:161
  187.9 8.0 %fusion.58 = f32[1024,1024]{1,0:T(8,128)} fusion(f32[1024,1024]{1,0:T(8,128)} %fusion.14, bf16[2,2048,1024]{2,1,0:T(8,128)(2,1)S(1)} %bitcast.268, s32[]{:T(128)S(6)} %select_n.164, bf16[512,2048]{1,0:T(8,128)(2,1)S(1)} %get-tuple-element.135, bf16[512,2048]{1,0:T(8,128)(2,1)S(1)} %get-tuple-element.136), kind=kOutput, calls=%fused_computation.103 | convolution fusion | flops 4304404480 | bytes 16777220 | tf_op jit(solution)/shard_map/dot_general | solution.py:161
  196.0 4.5 %slice_add_fusion.4 = (f32[512,512]{1,0:T(8,128)S(1)}, f32[512,512]{1,0:T(8,128)S(1)}, f32[512,512]{1,0:T(8,128)S(1)}, f32[512,512]{1,0:T(8,128)S(1)}, f32[512,5...) fusion(f32[1024,1024]{1,0:T(8,128)} %fusion.61, ...), kind=kLoop, calls=%fused_computation.245 | loop fusion | flops 3145728 | bytes 16777220 | tf_op jit(solution)/shard_map/add | solution.py:173
  200.4 3.9 %fusion.115 = f32[512,1024]{1,0:T(8,128)S(1)} fusion(f32[1024,512]{1,0:T(8,128)S(1)} %copy-done.1, f32[512]{0:T(512)S(1)} %copy-done.13, f32[512]{0:T(512)S(1)} %copy-done.8, f32[512,512]{1,0:T(8,128)S(1)} %get-tuple-element.35, f32[512,512]{1,0:T(8,128)S(1)} %get-tuple-element.34, f32[512,512]{1,0:T(8,128)S(1)} %get-tuple-element.33, ...), kind=kOutput, calls=%fused_computation.186 | convolution fusion | flops 1611923456 | bytes 8392704 | tf_op jit(solution)/shard_map/dot_general | solution.py:75
  204.4 3.9 %fusion.129 = f32[512,1024]{1,0:T(8,128)S(1)} fusion(f32[1024,512]{1,0:T(8,128)S(1)} %copy-done.1, f32[512]{0:T(512)S(1)} %copy-done.11, f32[512]{0:T(512)S(1)} %copy-done.9, f32[512,512]{1,0:T(8,128)S(1)} %get-tuple-element.35, f32[512,512]{1,0:T(8,128)S(1)} %get-tuple-element.34, f32[512,512]{1,0:T(8,128)S(1)} %get-tuple-element.33, ...), kind=kOutput, calls=%fused_computation.200 | convolution fusion | flops 1611923456 | bytes 8392704 | tf_op jit(solution)/shard_map/dot_general | solution.py:75
  208.3 4.2 %fusion.122 = f32[512,1024]{1,0:T(8,128)S(1)} fusion(f32[1024,512]{1,0:T(8,128)S(1)} %copy-done.1, f32[512]{0:T(512)S(1)} %copy-done.12, f32[512]{0:T(512)S(1)} %copy-done.10, f32[512,512]{1,0:T(8,128)S(1)} %get-tuple-element.38, f32[512,512]{1,0:T(8,128)S(1)} %get-tuple-element.37, f32[512,512]{1,0:T(8,128)S(1)} %get-tuple-element.39, ...), kind=kOutput, calls=%fused_computation.193 | convolution fusion | flops 1611923456 | bytes 8392704 | tf_op jit(solution)/shard_map/dot_general | solution.py:75
  212.4 3.6 fusion.135
  216.1 3.9 %add_bitcast_fusion.4 = f32[1024,512]{0,1:T(8,128)S(1)} fusion(f32[512,1024]{1,0:T(8,128)S(1)} %fusion.115, f32[1024,512]{1,0:T(8,128)S(1)} %copy-done, f32[512]{0:T(512)S(1)} %copy-done.13, f32[512]{0:T(512)S(1)} %copy-done.8, f32[512,512]{1,0:T(8,128)S(1)} %get-tuple-element.35, f32[512,512]{1,0:T(8,128)S(1)} %get-tuple-element.34, ...), kind=kOutput, calls=%fused_computation.79 | convolution fusion | flops 1612447744 | bytes 10489856 | tf_op jit(solution)/shard_map/dot_general | solution.py:75
  220.1 4.0 %add_bitcast_fusion.5 = f32[1024,512]{0,1:T(8,128)S(1)} fusion(f32[512,1024]{1,0:T(8,128)S(1)} %fusion.122, f32[1024,512]{1,0:T(8,128)S(1)} %copy-done, f32[512]{0:T(512)S(1)} %copy-done.12, f32[512]{0:T(512)S(1)} %copy-done.10, f32[512,512]{1,0:T(8,128)S(1)} %get-tuple-element.38, f32[512,512]{1,0:T(8,128)S(1)} %get-tuple-element.37, ...), kind=kOutput, calls=%fused_computation.80 | convolution fusion | flops 1612447744 | bytes 10489856 | tf_op jit(solution)/shard_map/dot_general | solution.py:75
  224.1 4.1 %add_bitcast_fusion.6 = f32[1024,512]{0,1:T(8,128)S(1)} fusion(f32[512,1024]{1,0:T(8,128)S(1)} %fusion.129, f32[1024,512]{1,0:T(8,128)S(1)} %copy-done, f32[512]{0:T(512)S(1)} %copy-done.11, f32[512]{0:T(512)S(1)} %copy-done.9, f32[512,512]{1,0:T(8,128)S(1)} %get-tuple-element.35, f32[512,512]{1,0:T(8,128)S(1)} %get-tuple-element.34, ...), kind=kOutput, calls=%fused_computation.81 | convolution fusion | flops 1612447744 | bytes 10489856 | tf_op jit(solution)/shard_map/dot_general | solution.py:75
  228.2 3.6 add_bitcast_fusion.7
  238.2 3.2 fusion.83
  241.4 2.8 add_bitcast_fusion.1
  244.2 2.8 fusion.72
  247.0 2.8 add_bitcast_fusion
  250.8 2.9 fusion.105
  253.8 2.8 add_bitcast_fusion.3
  256.6 2.8 fusion.94
  259.4 2.8 add_bitcast_fusion.2
  263.3 3.5 fusion.36
  268.4 1.6 collective-permute-start.9
  270.5 24.3 %collective-permute-done.10 = f32[2,4,1024]{2,1,0:T(4,128)S(1)} collective-permute-done((f32[2,4,1024]{2,1,0:T(4,128)S(1)}, f32[2,4,1024]{2,1,0:T(4,128)S(1)}, u32[]{:S(2)}, u32[]{:S(2)}) %collective-permute-start.10) | collective-permute-done | bytes 32800 | tf_op jit(solution)/shard_map/ppermute | solution.py:22
  295.7 2.3 slice_add_fusion.1
  298.0 1.1 dynamic-slice_bitcast_fusion.5
  299.1 1.5 collective-permute-start.12
  301.1 6.4 %fusion.6 = f32[256,2048]{1,0:T(8,128)S(1)} fusion(f32[2,1024,2048]{2,1,0:T(8,128)} %constant.220.clone, s32[]{:T(128)S(6)} %select_n.188, f32[2,256,1024]{2,1,0:T(8,128)S(1)} %slice_add_fusion.1), kind=kOutput, calls=%fused_computation.7 | convolution fusion | flops 3221225472 | bytes 11535360 | tf_op jit(solution)/shard_map/dot_general | solution.py:275
  307.6 6.9 %bitcast_reduce_fusion.1 = (f32[4,2048]{1,0:T(4,128)S(1)}, f32[256,2048]{1,0:T(8,128)S(1)}) fusion(f32[256,2048]{1,0:T(8,128)S(1)} %fusion.6, f32[256,1024]{1,0:T(8,128)} %collective-permute-done.11, f32[2,1024,2048]{2,1,0:T(8,128)} %constant.220.clone, s32[]{:T(128)S(6)} %select_n.192), kind=kOutput, calls=%fused_computation.64 | convolution fusion | flops 3222790144 | bytes 13664260 | tf_op jit(solution)/shard_map/dot_general | solution.py:275
  314.5 10.9 %collective-permute-done.13 = f32[2,4,1024]{2,1,0:T(4,128)S(1)} collective-permute-done((f32[2,4,1024]{2,1,0:T(4,128)S(1)}, f32[2,4,1024]{2,1,0:T(4,128)S(1)}, u32[]{:S(2)}, u32[]{:S(2)}) %collective-permute-start.13) | collective-permute-done | bytes 32800 | tf_op jit(solution)/shard_map/ppermute | solution.py:22
  325.4 1.9 slice_add_fusion
  328.2 2.0 collective-permute-done.14
  330.2 4.7 %fusion = f32[256,2048]{1,0:T(8,128)S(1)} fusion(f32[256,1024]{1,0:T(8,128)S(1)} %collective-permute-done.14, f32[2,1024,2048]{2,1,0:T(8,128)S(1)} %bitcast.240, s32[]{:T(128)S(6)} %select_n.192), kind=kOutput, calls=%fused_computation.1 | convolution fusion | flops 3221225472 | bytes 11534340 | tf_op jit(solution)/shard_map/dot_general | solution.py:275
  334.8 4.5 %bitcast_reduce_fusion = (f32[4,2048]{1,0:T(4,128)S(1)}, f32[256,2048]{1,0:T(8,128)S(1)}) fusion(f32[256,2048]{1,0:T(8,128)S(1)} %fusion, f32[2,1024,2048]{2,1,0:T(8,128)S(1)} %bitcast.240, s32[]{:T(128)S(6)} %select_n.188, f32[2,256,1024]{2,1,0:T(8,128)S(1)} %slice_add_fusion), kind=kOutput, calls=%fused_computation.59 | convolution fusion | flops 3222790144 | bytes 13665280 | tf_op jit(solution)/shard_map/dot_general | solution.py:275
  340.5 2.2 collective-permute-start.18
  343.2 35.8 %collective-permute-done.16 = f32[4,2048]{1,0:T(4,128)S(1)} collective-permute-done((f32[4,2048]{1,0:T(4,128)S(1)}, f32[4,2048]{1,0:T(4,128)S(1)}, u32[]{:S(2)}, u32[]{:S(2)}) %collective-permute-start.16) | collective-permute-done | bytes 32800 | tf_op jit(solution)/shard_map/ppermute | solution.py:17
  380.1 4.0 %maximum_bitcast_fusion = f32[1,2,512,2048]{3,2,1,0:T(8,128)} fusion(f32[1,512,2048]{2,1,0:T(8,128)S(1)} %maximum_bitcast_fusion.2, f32[1,512,2048]{2,1,0:T(8,128)S(1)} %maximum_bitcast_fusion.1), kind=kLoop, calls=%fused_computation | loop fusion | flops 2097152 | bytes 16777216 | tf_op jit(solution)/shard_map/broadcast_in_dim | solution.py:279
  (147 shorter events, 20.9 us)
Async XLA Ops:
  2.6 8.6 %copy-start.17 = (s32[1,3]{1,0:T(1,128)S(1)}, s32[1,3]{1,0:T(1,128)}, u32[]{:S(2)}) copy-start(s32[1,3]{1,0:T(1,128)} %param.43) | copy-start | bytes 40
  6.6 49.7 %collective-permute-start.1 = (bf16[512,2048]{1,0:T(8,128)(2,1)}, bf16[512,2048]{1,0:T(8,128)(2,1)}, u32[]{:S(2)}, u32[]{:S(2)}) collective-permute-start(bf16[512,2048]{1,0:T(8,128)(2,1)} %get-tuple-element.60), channel_id=1, source_target_pairs={{0,8},{4,12},{8,0},{12,4},{1,9},{5,13},{9,1},{13,5},{2,10},{6,14},... | collective-permute-start | bytes 6291464 | tf_op jit(solution)/shard_map/ppermute | solution.py:22
  9.6 46.8 %collective-permute-start = (bf16[512,2048]{1,0:T(8,128)(2,1)S(1)}, bf16[512,2048]{1,0:T(8,128)(2,1)}, u32[]{:S(2)}, u32[]{:S(2)}) collective-permute-start(bf16[512,2048]{1,0:T(8,128)(2,1)S(1)} %get-tuple-element.59), channel_id=1, source_target_pairs={{0,4},{4,0},{8,12},{12,8},{1,5},{5,1},{9,13},{13,9},{2,6},{6,2},{1... | collective-permute-start | bytes 6291464 | tf_op jit(solution)/shard_map/ppermute | solution.py:31
  9.6 6.5 %collective-permute-start.3 = (s32[1,1]{1,0:T(1,128)}, s32[1,1]{1,0:T(1,128)}, u32[]{:S(2)}, u32[]{:S(2)}) collective-permute-start(s32[1,1]{1,0:T(1,128)} %get-tuple-element.125), channel_id=1, source_target_pairs={{0,1},{1,2},{2,3},{3,0},{4,5},{5,6},{6,7},{7,4},{8,9},{9,10},{10,1... | collective-permute-start | bytes 20 | tf_op jit(solution)/shard_map/ppermute | solution.py:17
  19.9 80.6 %collective-permute-start.6 = (bf16[512,2048]{1,0:T(8,128)(2,1)S(1)}, bf16[512,2048]{1,0:T(8,128)(2,1)}, u32[]{:S(2)}, u32[]{:S(2)}) collective-permute-start(bf16[512,2048]{1,0:T(8,128)(2,1)S(1)} %get-tuple-element.66), channel_id=1, source_target_pairs={{0,8},{4,12},{8,0},{12,4},{1,9},{5,13},{9,1},{13,5},{2,10},{6,14},... | collective-permute-start | bytes 6291464 | tf_op jit(solution)/shard_map/ppermute | solution.py:22
  20.5 83.8 %collective-permute-start.4 = (bf16[512,2048]{1,0:T(8,128)(2,1)S(1)}, bf16[512,2048]{1,0:T(8,128)(2,1)}, u32[]{:S(2)}, u32[]{:S(2)}) collective-permute-start(bf16[512,2048]{1,0:T(8,128)(2,1)S(1)} %get-tuple-element.65), channel_id=1, source_target_pairs={{0,3},{1,0},{2,1},{3,2},{4,7},{5,4},{6,5},{7,6},{8,11},{9,8},{10,9... | collective-permute-start | bytes 6291464 | tf_op jit(solution)/shard_map/ppermute | solution.py:17
  56.4 47.9 %collective-permute-start.2 = (bf16[512,2048]{1,0:T(8,128)(2,1)}, bf16[512,2048]{1,0:T(8,128)(2,1)S(1)}, u32[]{:S(2)}, u32[]{:S(2)}) collective-permute-start(bf16[512,2048]{1,0:T(8,128)(2,1)} %collective-permute-done.1), channel_id=1, source_target_pairs={{0,4},{4,0},{8,12},{12,8},{1,5},{5,1},{9,13},{13,9},{2,6},{6,2},{1... | collective-permute-start | bytes 6291464 | tf_op jit(solution)/shard_map/ppermute | solution.py:31
  56.4 8.5 %slice-start.4 = ((s8[8388608]{0:T(1024)(128)(4,1)}), s8[4194304]{0:T(1024)(128)(4,1)S(1)}, s32[]{:S(2)}) async-start(s8[8388608]{0:T(1024)(128)(4,1)} %bitcast.265), calls=%async_computation.4 | async-start | bytes 8388608
  58.4 6.5 %slice-start.5 = ((s8[8388608]{0:T(1024)(128)(4,1)}), s8[4194304]{0:T(1024)(128)(4,1)S(1)}, s32[]{:S(2)}) async-start(s8[8388608]{0:T(1024)(128)(4,1)} %bitcast.265), calls=%async_computation.5 | async-start | bytes 8388608
  100.5 50.4 %collective-permute-start.7 = (bf16[512,2048]{1,0:T(8,128)(2,1)}, bf16[512,2048]{1,0:T(8,128)(2,1)}, u32[]{:S(2)}, u32[]{:S(2)}) collective-permute-start(bf16[512,2048]{1,0:T(8,128)(2,1)} %collective-permute-done.6), channel_id=1, source_target_pairs={{0,3},{1,0},{2,1},{3,2},{4,7},{5,4},{6,5},{7,6},{8,11},{9,8},{10,9... | collective-permute-start | bytes 6291464 | tf_op jit(solution)/shard_map/ppermute | solution.py:17
  104.3 49.7 %collective-permute-start.5 = (bf16[512,2048]{1,0:T(8,128)(2,1)}, bf16[512,2048]{1,0:T(8,128)(2,1)}, u32[]{:S(2)}, u32[]{:S(2)}) collective-permute-start(bf16[512,2048]{1,0:T(8,128)(2,1)} %collective-permute-done.4), channel_id=1, source_target_pairs={{0,4},{4,0},{8,12},{12,8},{1,5},{5,1},{9,13},{13,9},{2,6},{6,2},{1... | collective-permute-start | bytes 6291464 | tf_op jit(solution)/shard_map/ppermute | solution.py:31
  117.5 1.6 copy-start.1
  117.6 1.6 copy-start.8
  117.6 1.6 copy-start.13
  119.2 3.9 %copy-start = (f32[1024,512]{1,0:T(8,128)S(1)}, f32[1024,512]{1,0:T(8,128)}, u32[]{:S(2)}) copy-start(f32[1024,512]{1,0:T(8,128)} %constant.226) | copy-start | bytes 6291460
  127.1 4.1 %copy-start.10 = (f32[512]{0:T(512)S(1)}, f32[512]{0:T(512)}, u32[]{:S(2)}) copy-start(f32[512]{0:T(512)} %constant.229) | copy-start | bytes 6148
  127.1 4.1 %copy-start.12 = (f32[512]{0:T(512)S(1)}, f32[512]{0:T(512)}, u32[]{:S(2)}) copy-start(f32[512]{0:T(512)} %constant.230) | copy-start | bytes 6148
  131.2 4.0 %copy-start.9 = (f32[512]{0:T(512)S(1)}, f32[512]{0:T(512)}, u32[]{:S(2)}) copy-start(f32[512]{0:T(512)} %constant.227) | copy-start | bytes 6148
  131.2 4.0 %copy-start.11 = (f32[512]{0:T(512)S(1)}, f32[512]{0:T(512)}, u32[]{:S(2)}) copy-start(f32[512]{0:T(512)} %constant.228) | copy-start | bytes 6148
  142.9 8.6 %copy-start.5 = (f32[1024,512]{0,1:T(8,128)}, f32[1024,512]{0,1:T(8,128)S(1)}, u32[]{:S(2)}) copy-start(f32[1024,512]{0,1:T(8,128)S(1)} %add_bitcast_fusion.11) | copy-start | bytes 6291460
  146.9 4.6 %copy-start.4 = (f32[512,512]{1,0:T(8,128)S(1)}, f32[512,512]{1,0:T(8,128)}, u32[]{:S(2)}) copy-start(f32[512,512]{1,0:T(8,128)} %constant.213.clone) | copy-start | bytes 3145732
  150.9 1.9 copy-start.3
  150.9 4.6 %collective-permute-start.8 = (bf16[512,2048]{1,0:T(8,128)(2,1)}, bf16[512,2048]{1,0:T(8,128)(2,1)S(1)}, u32[]{:S(2)}, u32[]{:S(2)}) collective-permute-start(bf16[512,2048]{1,0:T(8,128)(2,1)} %collective-permute-done.7), channel_id=1, source_target_pairs={{0,4},{4,0},{8,12},{12,8},{1,5},{5,1},{9,13},{13,9},{2,6},{6,2},{1... | collective-permute-start | bytes 6291464 | tf_op jit(solution)/shard_map/ppermute | solution.py:31
  168.2 19.7 %slice-start.6 = ((s8[8388608]{0:T(1024)(128)(4,1)}), s8[4194304]{0:T(1024)(128)(4,1)S(1)}, s32[]{:S(2)}) async-start(s8[8388608]{0:T(1024)(128)(4,1)} %bitcast.267), calls=%async_computation.6 | async-start | bytes 8388608
  178.5 9.5 %slice-start.7 = ((s8[8388608]{0:T(1024)(128)(4,1)}), s8[4194304]{0:T(1024)(128)(4,1)S(1)}, s32[]{:S(2)}) async-start(s8[8388608]{0:T(1024)(128)(4,1)} %bitcast.267), calls=%async_computation.7 | async-start | bytes 8388608
  231.9 2.5 copy-start.6
  235.9 0.7 copy-start.14
  235.9 2.3 copy-start.18
  235.9 2.3 copy-start.19
  235.9 2.3 copy-start.22
  235.9 2.3 copy-start.23
  238.2 3.2 copy-start.21
  247.0 2.8 copy-start.15
  247.0 2.8 copy-start.16
  259.3 2.8 copy-start.20
  268.4 26.4 %collective-permute-start.9 = (s16[2,256,1024]{2,1,0:T(8,128)(2,1)S(1)}, s16[2,256,1024]{2,1,0:T(8,128)(2,1)S(1)}, u32[]{:S(2)}, u32[]{:S(2)}) collective-permute-start(s16[2,256,1024]{2,1,0:T(8,128)(2,1)S(1)} %get-tuple-element.47), channel_id=1, source_target_pairs={{0,8},{4,12},{8,0},{12,4},{1,9},{5,13},{9,1},{13,5},{2,10},{6,14},... | collective-permute-start | bytes 3145736 | tf_op jit(solution)/shard_map/ppermute | solution.py:22
  270.0 24.8 %collective-permute-start.10 = (f32[2,4,1024]{2,1,0:T(4,128)S(1)}, f32[2,4,1024]{2,1,0:T(4,128)S(1)}, u32[]{:S(2)}, u32[]{:S(2)}) collective-permute-start(f32[2,4,1024]{2,1,0:T(4,128)S(1)} %get-tuple-element.89), channel_id=1, source_target_pairs={{0,8},{4,12},{8,0},{12,4},{1,9},{5,13},{9,1},{13,5},{2,10},{6,14},... | collective-permute-start | bytes 98312 | tf_op jit(solution)/shard_map/ppermute | solution.py:22
  294.8 0.9 copy-start.7
  299.1 8.5 %collective-permute-start.11 = (f32[256,1024]{1,0:T(8,128)}, f32[256,1024]{1,0:T(8,128)}, u32[]{:S(2)}, u32[]{:S(2)}) collective-permute-start(f32[256,1024]{1,0:T(8,128)} %dynamic-slice_bitcast_fusion.5), channel_id=1, source_target_pairs={{0,4},{4,0},{8,12},{12,8},{1,5},{5,1},{9,13},{13,9},{2,6},{6,2},{1... | collective-permute-start | bytes 3145736 | tf_op jit(solution)/shard_map/ppermute | solution.py:31
  299.1 26.3 %collective-permute-start.12 = (s16[2,256,1024]{2,1,0:T(8,128)(2,1)S(1)}, s16[2,256,1024]{2,1,0:T(8,128)(2,1)}, u32[]{:S(2)}, u32[]{:S(2)}) collective-permute-start(s16[2,256,1024]{2,1,0:T(8,128)(2,1)S(1)} %get-tuple-element.10), channel_id=1, source_target_pairs={{0,8},{4,12},{8,0},{12,4},{1,9},{5,13},{9,1},{13,5},{2,10},{6,14},... | collective-permute-start | bytes 3145736 | tf_op jit(solution)/shard_map/ppermute | solution.py:22
  300.6 24.8 %collective-permute-start.13 = (f32[2,4,1024]{2,1,0:T(4,128)S(1)}, f32[2,4,1024]{2,1,0:T(4,128)S(1)}, u32[]{:S(2)}, u32[]{:S(2)}) collective-permute-start(f32[2,4,1024]{2,1,0:T(4,128)S(1)} %get-tuple-element.11), channel_id=1, source_target_pairs={{0,8},{4,12},{8,0},{12,4},{1,9},{5,13},{9,1},{13,5},{2,10},{6,14},... | collective-permute-start | bytes 98312 | tf_op jit(solution)/shard_map/ppermute | solution.py:22
  301.1 29.0 %slice-start = ((s8[16777216]{0:T(1024)(128)(4,1)}), s8[4194304]{0:T(1024)(128)(4,1)S(1)}, s32[]{:S(2)}) async-start(s8[16777216]{0:T(1024)(128)(4,1)} %bitcast.239), calls=%async_computation | async-start | bytes 8388608
  301.1 29.0 %slice-start.1 = ((s8[16777216]{0:T(1024)(128)(4,1)}), s8[4194304]{0:T(1024)(128)(4,1)S(1)}, s32[]{:S(2)}) async-start(s8[16777216]{0:T(1024)(128)(4,1)} %bitcast.239), calls=%async_computation.1 | async-start | bytes 8388608
  307.6 17.8 %copy-start.2 = (f32[2,512,1024]{2,1,0:T(8,128)S(1)}, f32[2,512,1024]{2,1,0:T(8,128)}, u32[]{:S(2)}) copy-start(f32[2,512,1024]{2,1,0:T(8,128)} %get-tuple-element.23) | copy-start | bytes 12582916
  307.6 22.6 %slice-start.2 = ((s8[16777216]{0:T(1024)(128)(4,1)}), s8[4194304]{0:T(1024)(128)(4,1)S(1)}, s32[]{:S(2)}) async-start(s8[16777216]{0:T(1024)(128)(4,1)} %bitcast.239), calls=%async_computation.2 | async-start | bytes 8388608
  325.4 4.8 %slice-start.3 = ((s8[16777216]{0:T(1024)(128)(4,1)}), s8[4194304]{0:T(1024)(128)(4,1)S(1)}, s32[]{:S(2)}) async-start(s8[16777216]{0:T(1024)(128)(4,1)} %bitcast.239), calls=%async_computation.3 | async-start | bytes 8388608
  327.4 2.7 collective-permute-start.14
  327.8 51.2 %collective-permute-start.15 = (s16[256,2048]{1,0:T(8,128)(2,1)S(1)}, s16[256,2048]{1,0:T(8,128)(2,1)S(1)}, u32[]{:S(2)}, u32[]{:S(2)}) collective-permute-start(s16[256,2048]{1,0:T(8,128)(2,1)S(1)} %fusion.47), channel_id=1, source_target_pairs={{0,1},{1,2},{2,3},{3,0},{4,5},{5,6},{6,7},{7,4},{8,9},{9,10},{10,1... | collective-permute-start | bytes 3145736 | tf_op jit(solution)/shard_map/ppermute | solution.py:17
  339.7 39.7 %collective-permute-start.17 = (s16[256,2048]{1,0:T(8,128)(2,1)S(1)}, s16[256,2048]{1,0:T(8,128)(2,1)S(1)}, u32[]{:S(2)}, u32[]{:S(2)}) collective-permute-start(s16[256,2048]{1,0:T(8,128)(2,1)S(1)} %fusion.45), channel_id=1, source_target_pairs={{0,1},{1,2},{2,3},{3,0},{4,5},{5,6},{6,7},{7,4},{8,9},{9,10},{10,1... | collective-permute-start | bytes 3145736 | tf_op jit(solution)/shard_map/ppermute | solution.py:17
  339.8 39.3 %collective-permute-start.16 = (f32[4,2048]{1,0:T(4,128)S(1)}, f32[4,2048]{1,0:T(4,128)S(1)}, u32[]{:S(2)}, u32[]{:S(2)}) collective-permute-start(f32[4,2048]{1,0:T(4,128)S(1)} %get-tuple-element.85), channel_id=1, source_target_pairs={{0,1},{1,2},{2,3},{3,0},{4,5},{5,6},{6,7},{7,4},{8,9},{9,10},{10,1... | collective-permute-start | bytes 98312 | tf_op jit(solution)/shard_map/ppermute | solution.py:17
  340.5 38.9 %collective-permute-start.18 = (f32[4,2048]{1,0:T(4,128)S(1)}, f32[4,2048]{1,0:T(4,128)S(1)}, u32[]{:S(2)}, u32[]{:S(2)}) collective-permute-start(f32[4,2048]{1,0:T(4,128)S(1)} %get-tuple-element.87), channel_id=1, source_target_pairs={{0,1},{1,2},{2,3},{3,0},{4,5},{5,6},{6,7},{7,4},{8,9},{9,10},{10,1... | collective-permute-start | bytes 98312 | tf_op jit(solution)/shard_map/ppermute | solution.py:17
